TPU v7x, 512 devices: a whole 4x8x8 slice. The times are simulated.
512 devices in a mesh: section: 16 (over y, core), tensor: 4 (over z_hi), seq: 8 (over z_lo, x).
Axes of the slice: x: 4, y: 8, z: 8 (z_hi: 4, z_lo: 2; z = z_hi * 2 + z_lo), core: 2. Of those that a mesh axis runs over, the one named last changes fastest.
Arguments:
- queries: bfloat16 [16, 2048, 4096], P('section', 'seq', 'tensor'), may hold values from -6 to 6
- keys: bfloat16 [16, 2048, 512], P('section', 'seq', 'tensor'), may hold values from -6 to 6
- values: bfloat16 [16, 2048, 512], P('section', 'seq', 'tensor'), may hold values from -6 to 6
- cotangent: bfloat16 [16, 2048, 4096], P('section', 'seq', 'tensor'), may hold values from -6 to 6
- positions: int32 [2048], replicated, may hold values from 0 to 2047, as said below
Outputs:
- attn_out: bfloat16 [16, 2048, 4096], P('section', 'seq', 'tensor')
- grad_q: bfloat16 [16, 2048, 4096], P('section', 'seq', 'tensor')
- grad_k: bfloat16 [16, 2048, 512], P('section', 'seq', 'tensor')
- grad_v: bfloat16 [16, 2048, 512], P('section', 'seq', 'tensor')
Inputs may be any that keep to these rules, and one draw needn't show every extreme that they name: A permutation of 0 to 2047 in which every aligned block of 64 entries holds consecutive rising positions that start at a multiple of 64.
All inputs are finite; a program needn't handle non-finite values.
Results may differ from a plain program's by a relative error of at most 0.024.
Values may be sent and summed in bfloat16 or wider, within the bound.
A program may use at most 64 MiB of HBM per device.

v0:
```python
import math

import jax
import jax.numpy as jnp
from jax import lax
from jax.sharding import PartitionSpec as P

HD = 128


def swapped(value, axis, apart):
    mask = 2**apart
    pairs = [(source, source ^ mask) for source in range(lax.axis_size(axis))]
    return lax.ppermute(value, axis, pairs)


def hop_bits():
    count = lax.axis_size("section").bit_length() - 1
    return list(range(count))


def key_blocks(piece, positions, carry, compute):
    rows = piece[0].shape[0]
    block = math.gcd(rows, 512)

    def step(index, state):
        offset = index * block
        parts = tuple((lax.dynamic_slice_in_dim(member, offset, block, 0) for member in piece))
        key_pos = lax.dynamic_slice_in_dim(positions, offset, block, 0)
        return compute(state, parts, key_pos, offset)

    return lax.fori_loop(0, rows // block, step, carry)


def forward(q, k, v, q_pos, positions):
    tok, width = q.shape
    kv_width = k.shape[1]
    heads_kv = kv_width // HD
    group = width // kv_width
    scale = HD ** (-0.5)
    qh = q.reshape(tok, heads_kv, group, HD)
    latest = jnp.max(q_pos)

    def block_scores(keys_block, key_pos):
        kb = keys_block.reshape(-1, heads_kv, HD)
        visible = key_pos[None, :] <= q_pos[:, None]
        scores = jnp.einsum("tkgd,skd->kgts", qh, kb, preferred_element_type=jnp.float32) * scale
        return (jnp.where(visible, scores, -1e30), visible)

    def stats(state, parts, key_pos, first):

        def stats_work(inner):
            top, total = inner
            scores, visible = block_scores(parts[0], key_pos)
            top_new = jnp.maximum(top, jnp.max(scores, axis=-1))
            weights = jnp.where(visible, jnp.exp(scores - top_new[..., None]), 0.0)
            total = total * jnp.exp(top - top_new) + jnp.sum(weights, axis=-1)
            return (top_new, total)

        return lax.cond(jnp.min(key_pos) > latest, lambda inner: inner, stats_work, state)

    init = (
        jnp.full((heads_kv, group, tok), -1e30, jnp.float32),
        jnp.zeros((heads_kv, group, tok), jnp.float32),
    )
    top, total = key_blocks((lax.all_gather(k, "seq", axis=0, tiled=True),), positions, init, stats)
    lse = top + jnp.log(total)

    def mix(acc, parts, key_pos, first):

        def mix_work(inner):
            scores, visible = block_scores(parts[0], key_pos)
            vb = parts[1].reshape(-1, heads_kv, HD)
            probs_b = jnp.where(visible, jnp.exp(scores - lse[..., None]), 0.0).astype(jnp.bfloat16)
            return inner + jnp.einsum(
                "kgts,skd->tkgd", probs_b, vb, preferred_element_type=jnp.float32
            )

        return lax.cond(jnp.min(key_pos) > latest, lambda inner: inner, mix_work, acc)

    acc = key_blocks(
        (
            lax.all_gather(k, "seq", axis=0, tiled=True),
            lax.all_gather(v, "seq", axis=0, tiled=True),
        ),
        positions,
        jnp.zeros((tok, heads_kv, group, HD), jnp.float32),
        mix,
    )
    out = acc.astype(jnp.bfloat16)
    return (out.reshape(tok, width), lse)


def backward(q, k, v, out, lse, cot, q_pos, positions):
    tok, width = q.shape
    kv_width = k.shape[1]
    heads_kv = kv_width // HD
    group = width // kv_width
    scale = HD ** (-0.5)
    seq_total = positions.shape[0]
    qh = q.reshape(tok, heads_kv, group, HD)
    doh = cot.reshape(tok, heads_kv, group, HD)
    outh = out.reshape(tok, heads_kv, group, HD)
    dvec = jnp.einsum("tkgd,tkgd->kgt", doh, outh, preferred_element_type=jnp.float32)
    latest = jnp.max(q_pos)

    def compute(state, parts, key_pos, first):

        def compute_work(inner):
            grad_acc, terms = inner
            kb = parts[0].reshape(-1, heads_kv, HD)
            vb = parts[1].reshape(-1, heads_kv, HD)
            visible = key_pos[None, :] <= q_pos[:, None]
            scores = (
                jnp.einsum("tkgd,skd->kgts", qh, kb, preferred_element_type=jnp.float32) * scale
            )
            probs = jnp.where(visible, jnp.exp(scores - lse[..., None]), 0.0)
            probs_b = probs.astype(jnp.bfloat16)
            dprobs = jnp.einsum("tkgd,skd->kgts", doh, vb, preferred_element_type=jnp.float32)
            dscores = (probs * (dprobs - dvec[..., None])).astype(jnp.bfloat16)
            grad_acc = grad_acc + jnp.einsum(
                "kgts,skd->tkgd", dscores, kb, preferred_element_type=jnp.float32
            )
            key_term = (
                jnp.einsum("kgts,tkgd->skd", dscores, qh, preferred_element_type=jnp.float32)
                * scale
            )
            value_term = jnp.einsum(
                "kgts,tkgd->skd", probs_b, doh, preferred_element_type=jnp.float32
            )
            block_rows = key_term.shape[0]
            joined = jnp.concatenate(
                [key_term.reshape(block_rows, kv_width), value_term.reshape(block_rows, kv_width)],
                axis=1,
            )
            terms = lax.dynamic_update_slice(terms, joined, (first, jnp.int32(0)))
            return (grad_acc, terms)

        return lax.cond(jnp.min(key_pos) > latest, lambda inner: inner, compute_work, state)

    init = (
        jnp.zeros((tok, heads_kv, group, HD), jnp.float32),
        jnp.zeros((seq_total, 2 * kv_width), jnp.float32),
    )
    grad_acc, terms = key_blocks(
        (
            lax.all_gather(k, "seq", axis=0, tiled=True),
            lax.all_gather(v, "seq", axis=0, tiled=True),
        ),
        positions,
        init,
        compute,
    )
    grad_q = (grad_acc * scale).astype(jnp.bfloat16).reshape(tok, width)
    rounded = lax.optimization_barrier(terms.astype(jnp.bfloat16)).astype(jnp.float32)
    summed = lax.psum_scatter(
        rounded.astype(jnp.bfloat16), "seq", scatter_dimension=0, tiled=True
    ).astype(jnp.float32)
    grad_k = summed[:, :kv_width].astype(jnp.bfloat16)
    grad_v = summed[:, kv_width:].astype(jnp.bfloat16)
    return (grad_q, grad_k, grad_v)


def local(queries, keys, values, cotangent, positions):
    q_here = queries[0]
    k_here = keys[0]
    v_here = values[0]
    cot_here = cotangent[0]
    tok = q_here.shape[0]
    q_pos = lax.dynamic_slice_in_dim(positions, lax.axis_index("seq") * tok, tok, 0)
    out, lse = forward(q_here, k_here, v_here, q_pos, positions)
    stash_q, stash_k, stash_v = (q_here, k_here, v_here)
    for bit in hop_bits():
        stash_q, stash_k, stash_v = swapped((stash_q, stash_k, stash_v), "section", bit)
    again, lse_again = forward(stash_q, stash_k, stash_v, q_pos, positions)
    grad_q, grad_k, grad_v = backward(
        stash_q, stash_k, stash_v, again, lse_again, cot_here, q_pos, positions
    )
    for bit in hop_bits():
        grad_q, grad_k, grad_v = swapped((grad_q, grad_k, grad_v), "section", bit)
    return (out[None], grad_q[None], grad_k[None], grad_v[None])


def solution(mesh):
    return jax.shard_map(
        local,
        mesh=mesh,
        in_specs=(
            P("section", "seq", "tensor"),
            P("section", "seq", "tensor"),
            P("section", "seq", "tensor"),
            P("section", "seq", "tensor"),
            P(),
        ),
        out_specs=(
            P("section", "seq", "tensor"),
            P("section", "seq", "tensor"),
            P("section", "seq", "tensor"),
            P("section", "seq", "tensor"),
        ),
        check_vma=False,
    )
```

profile of v0, /device:TPU:1, one launch (start us, length us, event | category | flops | bytes accessed | tf_op | source)
XLA Modules:
  0.0 397.1 jit_solution(1147348443433842185)
XLA Ops:
  7.2 8.8 %collective-permute-start.4 = (bf16[256,1024]{1,0:T(8,128)(2,1)}, bf16[256,1024]{1,0:T(8,128)(2,1)S(1)}, u32[]{:S(2)}, u32[]{:S(2)}) collective-permute-start(bf16[256,1024]{1,0:T(8,128)(2,1)} %bitcast.244), channel_id=1, source_target_pairs={{0,32},{32,0},{64,96},{96,64},{128,160},{160,128},{192,224},{224,1... | collective-permute-start | bytes 1572872 | tf_op jit(solution)/shard_map/ppermute | solution.py:14
  19.7 13.1 %collective-permute-done.5 = bf16[256,1024]{1,0:T(8,128)(2,1)S(1)} collective-permute-done((bf16[256,1024]{1,0:T(8,128)(2,1)S(1)}, bf16[256,1024]{1,0:T(8,128)(2,1)S(1)}, u32[]{:S(2)}, u32[]{:S(2)}) %collective-permute-start.5) | collective-permute-done | bytes 524320 | tf_op jit(solution)/shard_map/ppermute | solution.py:14
  34.7 3.1 collective-permute-start.8
  41.7 3.4 collective-permute-start.1
  46.5 5.4 %collective-permute-start.10 = (bf16[256,128]{1,0:T(8,128)(2,1)S(1)}, bf16[256,128]{1,0:T(8,128)(2,1)S(1)}, u32[]{:S(2)}, u32[]{:S(2)}) collective-permute-start(bf16[256,128]{1,0:T(8,128)(2,1)S(1)} %collective-permute-done.9), channel_id=1, source_target_pairs={{0,128},{32,160},{64,192},{96,224},{128,0},{160,32},{192,64},{224,... | collective-permute-start | bytes 196616 | tf_op jit(solution)/shard_map/ppermute | solution.py:14
  57.0 7.8 %collective-permute-done.10 = bf16[256,128]{1,0:T(8,128)(2,1)S(1)} collective-permute-done((bf16[256,128]{1,0:T(8,128)(2,1)S(1)}, bf16[256,128]{1,0:T(8,128)(2,1)S(1)}, u32[]{:S(2)}, u32[]{:S(2)}) %collective-permute-start.10) | collective-permute-done | bytes 65568 | tf_op jit(solution)/shard_map/ppermute | solution.py:14
  66.8 7.2 %collective-permute-start.7 = (bf16[256,1024]{1,0:T(8,128)(2,1)S(1)}, bf16[256,1024]{1,0:T(8,128)(2,1)S(1)}, u32[]{:S(2)}, u32[]{:S(2)}) collective-permute-start(bf16[256,1024]{1,0:T(8,128)(2,1)S(1)} %collective-permute-done.6), channel_id=1, source_target_pairs={{0,256},{32,288},{64,320},{96,352},{128,384},{160,416},{192,448},{... | collective-permute-start | bytes 1572872 | tf_op jit(solution)/shard_map/ppermute | solution.py:14
  77.5 25.6 %all_gather.19 = bf16[2048,128]{1,0:T(8,128)(2,1)S(1)} all-gather(bf16[256,128]{1,0:T(8,128)(2,1)S(1)} %collective-permute-done.11), channel_id=1, replica_groups=mesh['section'=16,'tensor'=4,'seq'=8] {'seq'}, dimensions={0}, use_global_device_ids=true | all-gather | bytes 589824 | tf_op jit(solution)/shard_map/all_gather | solution.py:148
  103.3 25.3 %all_gather.18 = bf16[2048,128]{1,0:T(8,128)(2,1)} all-gather(bf16[256,128]{1,0:T(8,128)(2,1)S(1)} %collective-permute-done.3), channel_id=1, replica_groups=mesh['section'=16,'tensor'=4,'seq'=8] {'seq'}, dimensions={0}, use_global_device_ids=true | all-gather | bytes 589824 | tf_op jit(solution)/shard_map/all_gather | solution.py:147
  131.0 20.1 %while.79 = (s32[]{:T(128)}, f32[1,8,256]{2,1,0:T(8,128)S(1)}, f32[1,8,256]{2,1,0:T(8,128)S(1)}, s32[2048]{0:T(1024)S(1)}, s32[]{:T(128)}, /*index=5*/s32[256]{0...) while((s32[]{:T(128)}, f32[1,8,256]{2,1,0:T(8,128)S(1)}, ...), condition=%wide.region_19.0_spmd, body=%wide.region_13.19_spmd.sunk | while | flops 276959744 | bytes 9551633 | solution.py:32
  133.1 2.9 conditional.12
  138.2 2.9 conditional.12
  143.2 2.9 conditional.12
  148.2 2.9 conditional.12
  151.2 19.3 %while.80 = (s32[]{:T(128)}, f32[256,1,8,128]{0,3,2,1:T(8,128)S(1)}, s32[2048]{0:T(1024)S(1)}, s32[]{:T(128)}, bf16[2048,128]{0,1:T(8,128)(2,1)S(1)}, /*index=5*...) while((s32[]{:T(128)}, ...), condition=%wide.region_24.0_spmd, body=%wide.region_20.24_spmd.sunk | while | flops 542507520 | bytes 3162377 | solution.py:32
  153.3 2.7 conditional.13
  153.5 2.6 fusion.46
  158.1 2.8 conditional.13
  158.3 2.6 fusion.46
  162.9 2.7 conditional.13
  163.1 2.6 fusion.46
  167.8 2.8 conditional.13
  167.9 2.6 fusion.46
  172.6 46.0 %while.81 = (s32[]{:T(128)}, f32[256,1,8,128]{0,3,2,1:T(8,128)S(1)}, bf16[2048,256]{0,1:T(8,128)(2,1)}, s32[2048]{0:T(1024)S(1)}, s32[]{:T(128)}, /*index=5*/bf1...) while((s32[]{:T(128)}, ...), condition=%wide.region_29.0_spmd, body=%wide.region_25.29_spmd.sunk | while | flops 1353712128 | bytes 26772384 | solution.py:32
  174.7 9.4 %conditional.14 = ((f32[256,1,8,128]{0,3,2,1:T(8,128)S(1)}, bf16[2048,256]{0,1:T(8,128)(2,1)})) conditional(s32[]{:T(128)} %convert_element_type.112, (bf16[2048,128]{1,0:T(8,128)(2,1)}, s32[]{:T(128)}, s32[512]{0:T(512)S(1)}, s32[256]{0:T(256)S(1)}, bf16[256,1,8,128]{0,3,2,1:T(8,128)(2,1)}, /*index=5*/f32[1,8,256]{2,1,0:T(8,128)S(1)}, ...), branch_computations={%region_27.27_spmd, %region_28.28_spmd} | conditional | flops 1353711616 | bytes 26767960 | solution.py:139
  176.7 2.3 fusion.63
  186.2 9.4 %conditional.14 = ((f32[256,1,8,128]{0,3,2,1:T(8,128)S(1)}, bf16[2048,256]{0,1:T(8,128)(2,1)})) conditional(s32[]{:T(128)} %convert_element_type.112, (bf16[2048,128]{1,0:T(8,128)(2,1)}, s32[]{:T(128)}, s32[512]{0:T(512)S(1)}, s32[256]{0:T(256)S(1)}, bf16[256,1,8,128]{0,3,2,1:T(8,128)(2,1)}, /*index=5*/f32[1,8,256]{2,1,0:T(8,128)S(1)}, ...), branch_computations={%region_27.27_spmd, %region_28.28_spmd} | conditional | flops 1353711616 | bytes 26767960 | solution.py:139
  188.2 2.3 fusion.63
  197.7 9.4 %conditional.14 = ((f32[256,1,8,128]{0,3,2,1:T(8,128)S(1)}, bf16[2048,256]{0,1:T(8,128)(2,1)})) conditional(s32[]{:T(128)} %convert_element_type.112, (bf16[2048,128]{1,0:T(8,128)(2,1)}, s32[]{:T(128)}, s32[512]{0:T(512)S(1)}, s32[256]{0:T(256)S(1)}, bf16[256,1,8,128]{0,3,2,1:T(8,128)(2,1)}, /*index=5*/f32[1,8,256]{2,1,0:T(8,128)S(1)}, ...), branch_computations={%region_27.27_spmd, %region_28.28_spmd} | conditional | flops 1353711616 | bytes 26767960 | solution.py:139
  199.7 2.3 fusion.63
  209.2 9.4 %conditional.14 = ((f32[256,1,8,128]{0,3,2,1:T(8,128)S(1)}, bf16[2048,256]{0,1:T(8,128)(2,1)})) conditional(s32[]{:T(128)} %convert_element_type.112, (bf16[2048,128]{1,0:T(8,128)(2,1)}, s32[]{:T(128)}, s32[512]{0:T(512)S(1)}, s32[256]{0:T(256)S(1)}, bf16[256,1,8,128]{0,3,2,1:T(8,128)(2,1)}, /*index=5*/f32[1,8,256]{2,1,0:T(8,128)S(1)}, ...), branch_computations={%region_27.27_spmd, %region_28.28_spmd} | conditional | flops 1353711616 | bytes 26767960 | solution.py:139
  211.2 2.3 fusion.63
  218.6 2.3 copy.45
  221.3 14.0 %collective-permute-start.12 = (bf16[256,1024]{1,0:T(8,128)(2,1)S(1)}, bf16[256,1024]{1,0:T(8,128)(2,1)S(1)}, u32[]{:S(2)}, u32[]{:S(2)}) collective-permute-start(bf16[256,1024]{1,0:T(8,128)(2,1)S(1)} %copy.63), channel_id=1, source_target_pairs={{0,32},{32,0},{64,96},{96,64},{128,160},{160,128},{192,224},{224,1... | collective-permute-start | bytes 1572872 | tf_op jit(solution)/shard_map/ppermute | solution.py:14
  239.5 23.7 %all-gather.1 = bf16[1,2048,128]{2,1,0:T(8,128)(2,1)S(1)} all-gather(bf16[1,256,128]{2,1,0:T(8,128)(2,1)S(1)} %copy-done.4), channel_id=3, replica_groups=mesh['section'=16,'tensor'=4,'seq'=8] {'seq'}, dimensions={1}, use_global_device_ids=true | all-gather | bytes 589824 | tf_op jit(solution)/shard_map/all_gather | solution.py:83
  263.1 4.4 %collective-permute-start.14 = (bf16[256,1024]{1,0:T(8,128)(2,1)S(1)}, bf16[256,1024]{1,0:T(8,128)(2,1)}, u32[]{:S(2)}, u32[]{:S(2)}) collective-permute-start(bf16[256,1024]{1,0:T(8,128)(2,1)S(1)} %collective-permute-done.13), channel_id=1, source_target_pairs={{0,128},{32,160},{64,192},{96,224},{128,0},{160,32},{192,64},{224,... | collective-permute-start | bytes 1572872 | tf_op jit(solution)/shard_map/ppermute | solution.py:14
  267.5 4.4 %reduce-scatter.2.cloned.1.call-done = bf16[256,256]{1,0:T(8,128)(2,1)} async-done(((bf16[2048,256]{1,0:T(8,128)(2,1)}), bf16[256,256]{1,0:T(8,128)(2,1)}) %reduce-scatter.2.cloned.1.call-update) | async-done | bytes 131088 | tf_op jit(solution)/shard_map/reduce_scatter | solution.py:156
  272.8 7.1 %collective-permute-start.16 = (bf16[256,128]{1,0:T(8,128)(2,1)S(1)}, bf16[256,128]{1,0:T(8,128)(2,1)S(1)}, u32[]{:S(2)}, u32[]{:S(2)}) collective-permute-start(bf16[256,128]{1,0:T(8,128)(2,1)S(1)} %get-tuple-element.1303), channel_id=1, source_target_pairs={{0,32},{32,0},{64,96},{96,64},{128,160},{160,128},{192,224},{224,1... | collective-permute-start | bytes 196616 | tf_op jit(solution)/shard_map/ppermute | solution.py:14
  281.9 16.3 %while.77 = (s32[]{:T(128)}, f32[1,8,256]{2,1,0:T(8,128)S(1)}, f32[1,8,256]{2,1,0:T(8,128)S(1)}, s32[2048]{0:T(1024)S(1)}, s32[]{:T(128)}, /*index=5*/s32[256]{0...) while((s32[]{:T(128)}, f32[1,8,256]{2,1,0:T(8,128)S(1)}, ...), condition=%wide.region_7.8_spmd, body=%wide.region_1.7_spmd.sunk | while | flops 276959744 | bytes 9551125 | solution.py:32
  298.4 3.2 collective-permute-start.17
  303.7 22.9 %all-gather = bf16[1,2048,128]{1,2,0:T(8,128)(2,1)S(1)} all-gather(bf16[1,256,128]{1,2,0:T(8,128)(2,1)S(1)} %copy.34), channel_id=2, replica_groups=mesh['section'=16,'tensor'=4,'seq'=8] {'seq'}, dimensions={1}, use_global_device_ids=true | all-gather | bytes 589824 | tf_op jit(solution)/shard_map/all_gather | solution.py:84
  326.6 7.1 %collective-permute-start.15 = (bf16[256,1024]{1,0:T(8,128)(2,1)}, bf16[256,1024]{1,0:T(8,128)(2,1)S(1)}, u32[]{:S(2)}, u32[]{:S(2)}) collective-permute-start(bf16[256,1024]{1,0:T(8,128)(2,1)} %collective-permute-done.14), channel_id=1, source_target_pairs={{0,256},{32,288},{64,320},{96,352},{128,384},{160,416},{192,448},{... | collective-permute-start | bytes 1572872 | tf_op jit(solution)/shard_map/ppermute | solution.py:14
  333.7 2.1 collective-permute-start.18
  335.9 4.1 %collective-permute-start.22 = (bf16[256,128]{1,0:T(8,128)(2,1)S(1)}, bf16[256,128]{1,0:T(8,128)(2,1)}, u32[]{:S(2)}, u32[]{:S(2)}) collective-permute-start(bf16[256,128]{1,0:T(8,128)(2,1)S(1)} %collective-permute-done.21), channel_id=1, source_target_pairs={{0,128},{32,160},{64,192},{96,224},{128,0},{160,32},{192,64},{224,... | collective-permute-start | bytes 196616 | tf_op jit(solution)/shard_map/ppermute | solution.py:14
  340.0 22.2 %collective-permute-done.18 = bf16[256,128]{1,0:T(8,128)(2,1)S(1)} collective-permute-done((bf16[256,128]{1,0:T(8,128)(2,1)S(1)}, bf16[256,128]{1,0:T(8,128)(2,1)S(1)}, u32[]{:S(2)}, u32[]{:S(2)}) %collective-permute-start.18) | collective-permute-done | bytes 65568 | tf_op jit(solution)/shard_map/ppermute | solution.py:14
  362.1 5.3 %collective-permute-start.19 = (bf16[256,128]{1,0:T(8,128)(2,1)S(1)}, bf16[256,128]{1,0:T(8,128)(2,1)S(1)}, u32[]{:S(2)}, u32[]{:S(2)}) collective-permute-start(bf16[256,128]{1,0:T(8,128)(2,1)S(1)} %collective-permute-done.18), channel_id=1, source_target_pairs={{0,256},{32,288},{64,320},{96,352},{128,384},{160,416},{192,448},{... | collective-permute-start | bytes 196616 | tf_op jit(solution)/shard_map/ppermute | solution.py:14
  367.5 3.9 collective-permute-start.23
  371.4 15.7 %while.78 = (s32[]{:T(128)}, f32[256,1,8,128]{0,3,2,1:T(8,128)S(1)}, s32[2048]{0:T(1024)S(1)}, s32[]{:T(128)}, bf16[2048,128]{0,1:T(8,128)(2,1)S(1)}, /*index=5*...) while((s32[]{:T(128)}, ...), condition=%wide.region_12.13_spmd, body=%wide.region_8.12_spmd.sunk | while | flops 542507520 | bytes 3162377 | solution.py:32
  (194 shorter events, 124.0 us)
Async XLA Ops:
  7.2 123.9 %copy-start.3 = (s32[2048]{0:T(1024)S(1)}, s32[2048]{0:T(1024)}, u32[]{:S(2)}) copy-start(s32[2048]{0:T(1024)} %param.29) | copy-start | bytes 24580
  7.2 264.7 %reduce-scatter.2.cloned.1.call-start = ((), (), s32[]{:S(2)}) async-start(), calls=%async_computation.1 | async-start | bytes 1179648 | tf_op jit(solution)/shard_map/reduce_scatter | solution.py:156
  7.2 10.5 %collective-permute-start.4 = (bf16[256,1024]{1,0:T(8,128)(2,1)}, bf16[256,1024]{1,0:T(8,128)(2,1)S(1)}, u32[]{:S(2)}, u32[]{:S(2)}) collective-permute-start(bf16[256,1024]{1,0:T(8,128)(2,1)} %bitcast.244), channel_id=1, source_target_pairs={{0,32},{32,0},{64,96},{96,64},{128,160},{160,128},{192,224},{224,1... | collective-permute-start | bytes 1572872 | tf_op jit(solution)/shard_map/ppermute | solution.py:14
  17.7 15.0 %collective-permute-start.5 = (bf16[256,1024]{1,0:T(8,128)(2,1)S(1)}, bf16[256,1024]{1,0:T(8,128)(2,1)S(1)}, u32[]{:S(2)}, u32[]{:S(2)}) collective-permute-start(bf16[256,1024]{1,0:T(8,128)(2,1)S(1)} %collective-permute-done.4), channel_id=1, source_target_pairs={{0,64},{32,96},{64,0},{96,32},{128,192},{160,224},{192,128},{224,1... | collective-permute-start | bytes 1572872 | tf_op jit(solution)/shard_map/ppermute | solution.py:14
  32.8 34.0 %collective-permute-start.6 = (bf16[256,1024]{1,0:T(8,128)(2,1)S(1)}, bf16[256,1024]{1,0:T(8,128)(2,1)S(1)}, u32[]{:S(2)}, u32[]{:S(2)}) collective-permute-start(bf16[256,1024]{1,0:T(8,128)(2,1)S(1)} %collective-permute-done.5), channel_id=1, source_target_pairs={{0,128},{32,160},{64,192},{96,224},{128,0},{160,32},{192,64},{224,... | collective-permute-start | bytes 1572872 | tf_op jit(solution)/shard_map/ppermute | solution.py:14
  34.7 5.1 %collective-permute-start.8 = (bf16[256,128]{1,0:T(8,128)(2,1)}, bf16[256,128]{1,0:T(8,128)(2,1)S(1)}, u32[]{:S(2)}, u32[]{:S(2)}) collective-permute-start(bf16[256,128]{1,0:T(8,128)(2,1)} %bitcast.248), channel_id=1, source_target_pairs={{0,32},{32,0},{64,96},{96,64},{128,160},{160,128},{192,224},{224,1... | collective-permute-start | bytes 196616 | tf_op jit(solution)/shard_map/ppermute | solution.py:14
  37.8 3.9 collective-permute-start
  39.7 6.7 %collective-permute-start.9 = (bf16[256,128]{1,0:T(8,128)(2,1)S(1)}, bf16[256,128]{1,0:T(8,128)(2,1)S(1)}, u32[]{:S(2)}, u32[]{:S(2)}) collective-permute-start(bf16[256,128]{1,0:T(8,128)(2,1)S(1)} %collective-permute-done.8), channel_id=1, source_target_pairs={{0,64},{32,96},{64,0},{96,32},{128,192},{160,224},{192,128},{224,1... | collective-permute-start | bytes 196616 | tf_op jit(solution)/shard_map/ppermute | solution.py:14
  41.7 13.4 %collective-permute-start.1 = (bf16[256,128]{1,0:T(8,128)(2,1)S(1)}, bf16[256,128]{1,0:T(8,128)(2,1)S(1)}, u32[]{:S(2)}, u32[]{:S(2)}) collective-permute-start(bf16[256,128]{1,0:T(8,128)(2,1)S(1)} %collective-permute-done), channel_id=1, source_target_pairs={{0,64},{32,96},{64,0},{96,32},{128,192},{160,224},{192,128},{224,1... | collective-permute-start | bytes 196616 | tf_op jit(solution)/shard_map/ppermute | solution.py:14
  46.5 18.3 %collective-permute-start.10 = (bf16[256,128]{1,0:T(8,128)(2,1)S(1)}, bf16[256,128]{1,0:T(8,128)(2,1)S(1)}, u32[]{:S(2)}, u32[]{:S(2)}) collective-permute-start(bf16[256,128]{1,0:T(8,128)(2,1)S(1)} %collective-permute-done.9), channel_id=1, source_target_pairs={{0,128},{32,160},{64,192},{96,224},{128,0},{160,32},{192,64},{224,... | collective-permute-start | bytes 196616 | tf_op jit(solution)/shard_map/ppermute | solution.py:14
  55.0 20.4 %collective-permute-start.2 = (bf16[256,128]{1,0:T(8,128)(2,1)S(1)}, bf16[256,128]{1,0:T(8,128)(2,1)S(1)}, u32[]{:S(2)}, u32[]{:S(2)}) collective-permute-start(bf16[256,128]{1,0:T(8,128)(2,1)S(1)} %collective-permute-done.1), channel_id=1, source_target_pairs={{0,128},{32,160},{64,192},{96,224},{128,0},{160,32},{192,64},{224,... | collective-permute-start | bytes 196616 | tf_op jit(solution)/shard_map/ppermute | solution.py:14
  64.8 12.7 %collective-permute-start.11 = (bf16[256,128]{1,0:T(8,128)(2,1)S(1)}, bf16[256,128]{1,0:T(8,128)(2,1)S(1)}, u32[]{:S(2)}, u32[]{:S(2)}) collective-permute-start(bf16[256,128]{1,0:T(8,128)(2,1)S(1)} %collective-permute-done.10), channel_id=1, source_target_pairs={{0,256},{32,288},{64,320},{96,352},{128,384},{160,416},{192,448},{... | collective-permute-start | bytes 196616 | tf_op jit(solution)/shard_map/ppermute | solution.py:14
  66.8 61.9 %collective-permute-start.7 = (bf16[256,1024]{1,0:T(8,128)(2,1)S(1)}, bf16[256,1024]{1,0:T(8,128)(2,1)S(1)}, u32[]{:S(2)}, u32[]{:S(2)}) collective-permute-start(bf16[256,1024]{1,0:T(8,128)(2,1)S(1)} %collective-permute-done.6), channel_id=1, source_target_pairs={{0,256},{32,288},{64,320},{96,352},{128,384},{160,416},{192,448},{... | collective-permute-start | bytes 1572872 | tf_op jit(solution)/shard_map/ppermute | solution.py:14
  75.5 27.9 %collective-permute-start.3 = (bf16[256,128]{1,0:T(8,128)(2,1)S(1)}, bf16[256,128]{1,0:T(8,128)(2,1)S(1)}, u32[]{:S(2)}, u32[]{:S(2)}) collective-permute-start(bf16[256,128]{1,0:T(8,128)(2,1)S(1)} %collective-permute-done.2), channel_id=1, source_target_pairs={{0,256},{32,288},{64,320},{96,352},{128,384},{160,416},{192,448},{... | collective-permute-start | bytes 196616 | tf_op jit(solution)/shard_map/ppermute | solution.py:14
  103.1 26.6 %copy-start = (bf16[2048,128]{1,0:T(8,128)(2,1)}, bf16[2048,128]{1,0:T(8,128)(2,1)S(1)}, u32[]{:S(2)}) copy-start(bf16[2048,128]{1,0:T(8,128)(2,1)S(1)} %all_gather.19) | copy-start | bytes 1572868
  174.7 2.0 copy-start.2
  186.2 2.0 copy-start.2
  197.7 2.0 copy-start.2
  209.2 2.0 copy-start.2
  218.6 20.3 %copy-start.1 = (bf16[1,256,1024]{2,1,0:T(8,128)(2,1)S(1)}, bf16[1,256,1024]{2,1,0:T(8,128)(2,1)}, u32[]{:S(2)}) copy-start(bf16[1,256,1024]{2,1,0:T(8,128)(2,1)} %param.25) | copy-start | bytes 1572868
  218.6 20.8 %copy-start.4 = (bf16[1,256,128]{2,1,0:T(8,128)(2,1)S(1)}, bf16[1,256,128]{2,1,0:T(8,128)(2,1)}, u32[]{:S(2)}) copy-start(bf16[1,256,128]{2,1,0:T(8,128)(2,1)} %param.26) | copy-start | bytes 196612
  221.3 15.5 %collective-permute-start.12 = (bf16[256,1024]{1,0:T(8,128)(2,1)S(1)}, bf16[256,1024]{1,0:T(8,128)(2,1)S(1)}, u32[]{:S(2)}, u32[]{:S(2)}) collective-permute-start(bf16[256,1024]{1,0:T(8,128)(2,1)S(1)} %copy.63), channel_id=1, source_target_pairs={{0,32},{32,0},{64,96},{96,64},{128,160},{160,128},{192,224},{224,1... | collective-permute-start | bytes 1572872 | tf_op jit(solution)/shard_map/ppermute | solution.py:14
  236.9 26.3 %collective-permute-start.13 = (bf16[256,1024]{1,0:T(8,128)(2,1)S(1)}, bf16[256,1024]{1,0:T(8,128)(2,1)S(1)}, u32[]{:S(2)}, u32[]{:S(2)}) collective-permute-start(bf16[256,1024]{1,0:T(8,128)(2,1)S(1)} %collective-permute-done.12), channel_id=1, source_target_pairs={{0,64},{32,96},{64,0},{96,32},{128,192},{160,224},{192,128},{224,1... | collective-permute-start | bytes 1572872 | tf_op jit(solution)/shard_map/ppermute | solution.py:14
  263.1 63.5 %collective-permute-start.14 = (bf16[256,1024]{1,0:T(8,128)(2,1)S(1)}, bf16[256,1024]{1,0:T(8,128)(2,1)}, u32[]{:S(2)}, u32[]{:S(2)}) collective-permute-start(bf16[256,1024]{1,0:T(8,128)(2,1)S(1)} %collective-permute-done.13), channel_id=1, source_target_pairs={{0,128},{32,160},{64,192},{96,224},{128,0},{160,32},{192,64},{224,... | collective-permute-start | bytes 1572872 | tf_op jit(solution)/shard_map/ppermute | solution.py:14
  272.8 25.6 %collective-permute-start.16 = (bf16[256,128]{1,0:T(8,128)(2,1)S(1)}, bf16[256,128]{1,0:T(8,128)(2,1)S(1)}, u32[]{:S(2)}, u32[]{:S(2)}) collective-permute-start(bf16[256,128]{1,0:T(8,128)(2,1)S(1)} %get-tuple-element.1303), channel_id=1, source_target_pairs={{0,32},{32,0},{64,96},{96,64},{128,160},{160,128},{192,224},{224,1... | collective-permute-start | bytes 196616 | tf_op jit(solution)/shard_map/ppermute | solution.py:14
  279.9 21.6 %collective-permute-start.20 = (bf16[256,128]{1,0:T(8,128)(2,1)S(1)}, bf16[256,128]{1,0:T(8,128)(2,1)S(1)}, u32[]{:S(2)}, u32[]{:S(2)}) collective-permute-start(bf16[256,128]{1,0:T(8,128)(2,1)S(1)} %get-tuple-element.1302), channel_id=1, source_target_pairs={{0,32},{32,0},{64,96},{96,64},{128,160},{160,128},{192,224},{224,1... | collective-permute-start | bytes 196616 | tf_op jit(solution)/shard_map/ppermute | solution.py:14
  281.9 16.4 %copy-start.5 = (bf16[1,256,128]{2,1,0:T(8,128)(2,1)S(1)}, bf16[1,256,128]{2,1,0:T(8,128)(2,1)}, u32[]{:S(2)}) copy-start(bf16[1,256,128]{2,1,0:T(8,128)(2,1)} %param.27) | copy-start | bytes 196612
  298.4 35.4 %collective-permute-start.17 = (bf16[256,128]{1,0:T(8,128)(2,1)S(1)}, bf16[256,128]{1,0:T(8,128)(2,1)S(1)}, u32[]{:S(2)}, u32[]{:S(2)}) collective-permute-start(bf16[256,128]{1,0:T(8,128)(2,1)S(1)} %collective-permute-done.16), channel_id=1, source_target_pairs={{0,64},{32,96},{64,0},{96,32},{128,192},{160,224},{192,128},{224,1... | collective-permute-start | bytes 196616 | tf_op jit(solution)/shard_map/ppermute | solution.py:14
  301.6 34.3 %collective-permute-start.21 = (bf16[256,128]{1,0:T(8,128)(2,1)S(1)}, bf16[256,128]{1,0:T(8,128)(2,1)S(1)}, u32[]{:S(2)}, u32[]{:S(2)}) collective-permute-start(bf16[256,128]{1,0:T(8,128)(2,1)S(1)} %collective-permute-done.20), channel_id=1, source_target_pairs={{0,64},{32,96},{64,0},{96,32},{128,192},{160,224},{192,128},{224,1... | collective-permute-start | bytes 196616 | tf_op jit(solution)/shard_map/ppermute | solution.py:14
  326.6 61.6 %collective-permute-start.15 = (bf16[256,1024]{1,0:T(8,128)(2,1)}, bf16[256,1024]{1,0:T(8,128)(2,1)S(1)}, u32[]{:S(2)}, u32[]{:S(2)}) collective-permute-start(bf16[256,1024]{1,0:T(8,128)(2,1)} %collective-permute-done.14), channel_id=1, source_target_pairs={{0,256},{32,288},{64,320},{96,352},{128,384},{160,416},{192,448},{... | collective-permute-start | bytes 1572872 | tf_op jit(solution)/shard_map/ppermute | solution.py:14
  333.7 28.4 %collective-permute-start.18 = (bf16[256,128]{1,0:T(8,128)(2,1)S(1)}, bf16[256,128]{1,0:T(8,128)(2,1)S(1)}, u32[]{:S(2)}, u32[]{:S(2)}) collective-permute-start(bf16[256,128]{1,0:T(8,128)(2,1)S(1)} %collective-permute-done.17), channel_id=1, source_target_pairs={{0,128},{32,160},{64,192},{96,224},{128,0},{160,32},{192,64},{224,... | collective-permute-start | bytes 196616 | tf_op jit(solution)/shard_map/ppermute | solution.py:14
  335.9 31.6 %collective-permute-start.22 = (bf16[256,128]{1,0:T(8,128)(2,1)S(1)}, bf16[256,128]{1,0:T(8,128)(2,1)}, u32[]{:S(2)}, u32[]{:S(2)}) collective-permute-start(bf16[256,128]{1,0:T(8,128)(2,1)S(1)} %collective-permute-done.21), channel_id=1, source_target_pairs={{0,128},{32,160},{64,192},{96,224},{128,0},{160,32},{192,64},{224,... | collective-permute-start | bytes 196616 | tf_op jit(solution)/shard_map/ppermute | solution.py:14
  362.1 26.1 %collective-permute-start.19 = (bf16[256,128]{1,0:T(8,128)(2,1)S(1)}, bf16[256,128]{1,0:T(8,128)(2,1)S(1)}, u32[]{:S(2)}, u32[]{:S(2)}) collective-permute-start(bf16[256,128]{1,0:T(8,128)(2,1)S(1)} %collective-permute-done.18), channel_id=1, source_target_pairs={{0,256},{32,288},{64,320},{96,352},{128,384},{160,416},{192,448},{... | collective-permute-start | bytes 196616 | tf_op jit(solution)/shard_map/ppermute | solution.py:14
  367.5 20.7 %collective-permute-start.23 = (bf16[256,128]{1,0:T(8,128)(2,1)}, bf16[256,128]{1,0:T(8,128)(2,1)S(1)}, u32[]{:S(2)}, u32[]{:S(2)}) collective-permute-start(bf16[256,128]{1,0:T(8,128)(2,1)} %collective-permute-done.22), channel_id=1, source_target_pairs={{0,256},{32,288},{64,320},{96,352},{128,384},{160,416},{192,448},{... | collective-permute-start | bytes 196616 | tf_op jit(solution)/shard_map/ppermute | solution.py:14
Sparse Core Ops, SparseCore 0:
  221.1 50.7 reduce-scatter.1
where the time goes:
time: 399 us; the launch traced here: 397 us
  starting transfers between devices  98.7 us (25%)
  blocking collectives  97.5 us (24%)
  matrix products  60.6 us (15%)
  waiting for transfers between devices  52.2 us (13%)
  other arithmetic  30.7 us (8%)
  loops' own time  28.2 us (7%)
  local copies, waits for them, and re-layouts  14.7 us (4%)
  between operations  14.6 us (4%)
    ppermute x24, starting transfers between devices, swapped(): return lax.ppermute(value, axis, pairs)  98.7 us
    ppermute x24, waiting for transfers between devices, swapped(): return lax.ppermute(value, axis, pairs)  47.8 us
    another operation x5, loops' own time, key_blocks(): return lax.fori_loop(0, rows // block, step, carry)  27.2 us
    all_gather x1, blocking collectives, backward(): lax.all_gather(v, 'seq', axis=0, tiled=True)  25.6 us
    all_gather x1, blocking collectives, backward(): lax.all_gather(k, 'seq', axis=0, tiled=True)  25.3 us
    all_gather x1, blocking collectives, forward(): lax.all_gather(k, 'seq', axis=0, tiled=True)  23.7 us
    all_gather x1, blocking collectives, forward(): lax.all_gather(v, 'seq', axis=0, tiled=True)  22.9 us
    dot_general x8, matrix products, mix_work(): jnp.einsum('kgts,skd->tkgd', probs_b, vb, preferred_element_type=jnp.floa...  17 us
  transfers between devices with their start and end apart: 25, of which 7 were waited for; matrix products, arithmetic and copies ran while one was open for 7% of the time, Pallas kernels for 0%

commit v1 on v0

v1 whole, which is shorter than its diff:
```python
import functools
import math

import jax
import jax.numpy as jnp
from jax import lax
from jax.experimental import pallas as pl
from jax.experimental.pallas import tpu as pltpu
from jax.sharding import PartitionSpec as P

HD = 128
MESH = pl.DeviceIdType.MESH
NT = (((1,), (1,)), ((), ()))
NN = (((1,), (0,)), ((), ()))
F32 = jnp.float32
BF16 = jnp.bfloat16


def dot(a, b, dims):
    return lax.dot_general(a, b, dims, preferred_element_type=F32)


def peers():
    section, tensor, seq = (lax.axis_index(a) for a in ("section", "tensor", "seq"))
    z, x = seq // 4, seq % 4
    found = []
    for slot in range(1, 8):
        dz, dx = slot // 4, slot % 4
        there = ((z + dz) % 2) * 4 + (x + dx) % 4
        back = dz * 4 + (4 - dx) % 4
        found.append((slot, back, (section, tensor, there)))
    return found


def greet(others):
    barrier = pltpu.get_barrier_semaphore()
    for _, _, device in others:
        pl.semaphore_signal(barrier, inc=1, device_id=device, device_id_type=MESH)
    pl.semaphore_wait(barrier, len(others))


def remote(src, dst, send, recv, device):
    return pltpu.make_async_remote_copy(
        src_ref=src, dst_ref=dst, send_sem=send, recv_sem=recv, device_id=device, device_id_type=MESH
    )


def fwd_kernel(
    heads, tok, q_hbm, k_hbm, v_hbm, pos_ref, o_ref, p_hbm, k_out, v_out, stat_ref,
    qst, kbuf, vbuf, scores, probs, otr, bias, top, total, qsem, ksend, krecv, vsend, vrecv, osem, psem,
):
    others = peers()
    loads = []
    for h in range(heads):
        loads.append(
            pltpu.make_async_copy(
                q_hbm.at[:, pl.ds(h * HD, HD)], qst.at[pl.ds(h * tok, tok), :], qsem.at[h]
            )
        )
    loads.append(pltpu.make_async_copy(k_hbm, kbuf.at[0], qsem.at[heads]))
    loads.append(pltpu.make_async_copy(v_hbm, vbuf.at[0], qsem.at[heads + 1]))
    for c in loads:
        c.start()
    greet(others)
    sends = []
    for slot, back, device in others:
        sends.append(remote(k_hbm, kbuf.at[back], ksend.at[slot], krecv.at[back], device))
    for slot, back, device in others:
        sends.append(remote(v_hbm, vbuf.at[back], vsend.at[slot], vrecv.at[back], device))
    for c in sends:
        c.start()
    for c in loads:
        c.wait()

    seq = lax.axis_index("seq")
    z, x = seq // 4, seq % 4
    q_row = pos_ref[pl.ds(seq, 1), :]
    rows = [
        pos_ref[pl.ds(((z + slot // 4) % 2) * 4 + (x + slot % 4) % 4, 1), :] for slot in range(8)
    ]
    k_cols = jnp.transpose(jnp.concatenate(rows, axis=0))
    for slot in range(8):
        visible = k_cols[:, slot : slot + 1] <= q_row
        bias[slot] = jnp.where(visible, 0.0, -1e30)
    top[...] = jnp.full_like(top, -1e30)
    total[...] = jnp.zeros_like(total)
    factor = HD**-0.5 * math.log2(math.e)

    def score(slot):
        kb = kbuf[slot]
        bb = bias[slot]
        for h in range(heads):
            part = dot(kb, qst[h * tok : (h + 1) * tok, :], NT) * factor + bb
            scores[slot, :, h * tok : (h + 1) * tok] = part
            top[h] = jnp.maximum(top[h], jnp.max(part.reshape(tok // 8, 8, tok), axis=0))

    score(0)

    def score_step(slot, carry):
        remote(kbuf.at[slot], kbuf.at[slot], ksend.at[slot], krecv.at[slot], others[0][2]).wait_recv()
        score(slot)
        return carry

    lax.fori_loop(1, 8, score_step, 0)
    for h in range(heads):
        top[h] = jnp.broadcast_to(jnp.max(top[h], axis=0, keepdims=True), (8, tok))

    otr[...] = jnp.zeros_like(otr)

    def mix(slot):
        vt = jnp.transpose(vbuf[slot])
        for h in range(heads):
            columns = slice(h * tok, (h + 1) * tok)
            raw = jnp.exp2(scores[slot, :, columns] - top[h, 0:1, :])
            total[h] += jnp.sum(raw.reshape(tok // 8, 8, tok), axis=0)
            pb = raw.astype(BF16)
            probs[slot, :, columns] = pb
            otr[:, columns] += dot(vt, pb, NN)
        pltpu.make_async_copy(probs.at[slot], p_hbm.at[slot], psem.at[slot]).start()

    mix(0)

    def mix_step(slot, carry):
        remote(vbuf.at[slot], vbuf.at[slot], vsend.at[slot], vrecv.at[slot], others[0][2]).wait_recv()
        mix(slot)
        return carry

    lax.fori_loop(1, 8, mix_step, 0)

    outs = [
        pltpu.make_async_copy(kbuf, k_out, osem.at[0]),
        pltpu.make_async_copy(vbuf, v_out, osem.at[1]),
    ]
    for c in outs:
        c.start()
    inverse = []
    for h in range(heads):
        columns = slice(h * tok, (h + 1) * tok)
        inv = 1.0 / jnp.sum(total[h], axis=0, keepdims=True)
        inverse.append(inv)
        o_ref[:, h * HD : (h + 1) * HD] = jnp.transpose(otr[:, columns] * inv).astype(BF16)
    stat_ref[...] = jnp.transpose(jnp.concatenate(inverse, axis=0))
    for c in sends:
        c.wait_send()
    for c in outs:
        c.wait()
    for slot in range(8):
        pltpu.make_async_copy(probs.at[slot], p_hbm.at[slot], psem.at[slot]).wait()


def bwd_kernel(
    heads, tok, q_hbm, cot_hbm, p_hbm, k_hbm, v_hbm, o_ref, stat_ref, gq_ref, gk_ref, gv_ref,
    qst, cst, probs, kbuf, vbuf, dst, dqt, sendbuf, recvbuf, own, qsem, psem, ksem, ssem, rsem,
):
    others = peers()
    scale = HD**-0.5
    loads = []
    for h in range(heads):
        loads.append(
            pltpu.make_async_copy(
                cot_hbm.at[:, pl.ds(h * HD, HD)], cst.at[pl.ds(h * tok, tok), :], qsem.at[h]
            )
        )
        loads.append(
            pltpu.make_async_copy(
                q_hbm.at[:, pl.ds(h * HD, HD)], qst.at[pl.ds(h * tok, tok), :], qsem.at[heads + h]
            )
        )
    loads.append(pltpu.make_async_copy(k_hbm, kbuf, ksem.at[0]))
    loads.append(pltpu.make_async_copy(v_hbm, vbuf, ksem.at[1]))
    for c in loads:
        c.start()
    for slot in range(8):
        pltpu.make_async_copy(p_hbm.at[slot], probs.at[slot], psem.at[slot]).start()
    greet(others)
    for c in loads:
        c.wait()

    columns = []
    for h in range(heads):
        rows = slice(h * tok, (h + 1) * tok)
        inv = stat_ref[:, h : h + 1]
        cot = cst[rows, :].astype(F32)
        columns.append(
            jnp.sum(cot * o_ref[:, h * HD : (h + 1) * HD].astype(F32), axis=1, keepdims=True) * inv
        )
        cst[rows, :] = (cot * inv).astype(BF16)
    dvec = jnp.transpose(jnp.concatenate(columns, axis=1))
    dqt[...] = jnp.zeros_like(dqt)

    def work(slot):
        pltpu.make_async_copy(p_hbm.at[slot], probs.at[slot], psem.at[slot]).wait()
        vb = vbuf[slot]
        kt = jnp.transpose(kbuf[slot])
        for h in range(heads):
            rows = slice(h * tok, (h + 1) * tok)
            dp = dot(vb, cst[rows, :], NT)
            ds = (probs[slot, :, rows].astype(F32) * (dp - dvec[h : h + 1, :])).astype(BF16)
            dst[:, rows] = ds
            dqt[:, rows] += dot(kt, ds, NN)
        dk = dot(dst[...], qst[...], NN) * scale
        dv = dot(probs[slot], cst[...], NN)
        return dk, dv

    def step(slot, carry):
        dk, dv = work(slot)
        sendbuf[slot, 0] = dk.astype(BF16)
        sendbuf[slot, 1] = dv.astype(BF16)
        dz, dx = slot // 4, slot % 4
        section, tensor, seq = (lax.axis_index(a) for a in ("section", "tensor", "seq"))
        z, x = seq // 4, seq % 4
        there = ((z + dz) % 2) * 4 + (x + dx) % 4
        back = dz * 4 + (4 - dx) % 4
        remote(
            sendbuf.at[slot], recvbuf.at[back], ssem.at[slot], rsem.at[back], (section, tensor, there)
        ).start()
        return carry

    lax.fori_loop(1, 8, step, 0)
    dk, dv = work(0)
    own[0] = dk
    own[1] = dv
    for h in range(heads):
        part = dqt[:, h * tok : (h + 1) * tok] * scale
        gq_ref[:, h * HD : (h + 1) * HD] = jnp.transpose(part).astype(BF16)
    for slot, back, device in others:
        remote(sendbuf.at[slot], recvbuf.at[slot], ssem.at[slot], rsem.at[slot], device).wait()
        own[0] += recvbuf[slot, 0].astype(F32)
        own[1] += recvbuf[slot, 1].astype(F32)
    gk_ref[...] = own[0].astype(BF16)
    gv_ref[...] = own[1].astype(BF16)


def local(queries, keys, values, cotangent, positions):
    q, k, v, cot = queries[0], keys[0], values[0], cotangent[0]
    tok, width = q.shape
    heads = width // HD
    wide = heads * tok
    count = lax.axis_size("section")
    mirrored = lax.ppermute(cot, "section", [(s, count - 1 - s) for s in range(count)])
    pos = positions.reshape(8, tok).astype(F32)
    anywhere = pl.BlockSpec(memory_space=pl.ANY)
    vmem = pl.BlockSpec(memory_space=pltpu.VMEM)
    dma = pltpu.SemaphoreType.DMA
    out, probs, k_all, v_all, stat = pl.pallas_call(
        functools.partial(fwd_kernel, heads, tok),
        out_shape=(
            jax.ShapeDtypeStruct((tok, width), BF16),
            jax.ShapeDtypeStruct((8, tok, wide), BF16),
            jax.ShapeDtypeStruct((8, tok, HD), BF16),
            jax.ShapeDtypeStruct((8, tok, HD), BF16),
            jax.ShapeDtypeStruct((tok, heads), F32),
        ),
        in_specs=[anywhere, anywhere, anywhere, vmem],
        out_specs=(vmem, anywhere, anywhere, anywhere, vmem),
        scratch_shapes=[
            pltpu.VMEM((wide, HD), BF16),
            pltpu.VMEM((8, tok, HD), BF16),
            pltpu.VMEM((8, tok, HD), BF16),
            pltpu.VMEM((8, tok, wide), F32),
            pltpu.VMEM((8, tok, wide), BF16),
            pltpu.VMEM((HD, wide), F32),
            pltpu.VMEM((8, tok, tok), F32),
            pltpu.VMEM((heads, 8, tok), F32),
            pltpu.VMEM((heads, 8, tok), F32),
            dma((heads + 2,)),
            dma((8,)),
            dma((8,)),
            dma((8,)),
            dma((8,)),
            dma((2,)),
            dma((8,)),
        ],
        cost_estimate=pl.CostEstimate(
            flops=4 * wide * 8 * tok * HD, bytes_accessed=2**24, transcendentals=wide * 8 * tok
        ),
        compiler_params=pltpu.CompilerParams(
            collective_id=1, has_side_effects=True, vmem_limit_bytes=48 * 2**20
        ),
    )(q, k, v, pos)
    grad_q, grad_k, grad_v = pl.pallas_call(
        functools.partial(bwd_kernel, heads, tok),
        out_shape=(
            jax.ShapeDtypeStruct((tok, width), BF16),
            jax.ShapeDtypeStruct((tok, HD), BF16),
            jax.ShapeDtypeStruct((tok, HD), BF16),
        ),
        in_specs=[anywhere] * 5 + [vmem] * 2,
        out_specs=(vmem, vmem, vmem),
        scratch_shapes=[
            pltpu.VMEM((wide, HD), BF16),
            pltpu.VMEM((wide, HD), BF16),
            pltpu.VMEM((8, tok, wide), BF16),
            pltpu.VMEM((8, tok, HD), BF16),
            pltpu.VMEM((8, tok, HD), BF16),
            pltpu.VMEM((tok, wide), BF16),
            pltpu.VMEM((HD, wide), F32),
            pltpu.VMEM((8, 2, tok, HD), BF16),
            pltpu.VMEM((8, 2, tok, HD), BF16),
            pltpu.VMEM((2, tok, HD), F32),
            dma((2 * heads,)),
            dma((8,)),
            dma((2,)),
            dma((8,)),
            dma((8,)),
        ],
        cost_estimate=pl.CostEstimate(
            flops=8 * wide * 8 * tok * HD, bytes_accessed=2**24, transcendentals=0
        ),
        compiler_params=pltpu.CompilerParams(
            collective_id=2, has_side_effects=True, vmem_limit_bytes=48 * 2**20
        ),
    )(q, mirrored, probs, k_all, v_all, out, stat)
    return (out[None], grad_q[None], grad_k[None], grad_v[None])


def solution(mesh):
    split = P("section", "seq", "tensor")
    return jax.shard_map(
        local,
        mesh=mesh,
        in_specs=(split, split, split, split, P()),
        out_specs=(split, split, split, split),
        check_vma=False,
    )
```

time: 399 us -> 64.7 us (0.16)
  the two profiles are of different devices: /device:TPU:1 before, /device:TPU:14 now
where the time goes in v1:
time: 64.7 us; the launch traced here: 64.3 us
  Pallas kernels  51.9 us (80%)
  local copies, waits for them, and re-layouts  5.57 us (9%)
  starting transfers between devices  5.49 us (8%)
  other arithmetic  0.7 us (1%)
  between operations  0.67 us (1%)
    pallas_call x1, Pallas kernels, local(): pl.pallas_call(functools.partial(bwd_kernel, heads, tok), out_shape=(jax....  29.1 us
    pallas_call x1, Pallas kernels, local(): pl.pallas_call(functools.partial(fwd_kernel, heads, tok), out_shape=(jax....  22.8 us
    unnamed x10, local copies, waits for them, and re-layouts  5.57 us
    ppermute x1, starting transfers between devices, local(): lax.ppermute(cot, 'section', [(s, count - 1 - s) for s in range(count)])  5.49 us
  transfers between devices with their start and end apart: 1, of which 0 were waited for; matrix products, arithmetic and copies ran while one was open for 1% of the time, Pallas kernels for 35%

profile of v1, /device:TPU:14, one launch (start us, length us, event | category | flops | bytes accessed | tf_op | source)
XLA Modules:
  0.0 64.3 jit_solution(6916265695290790591)
XLA Ops:
  0.6 5.5 %collective-permute-start = (bf16[256,1024]{1,0:T(8,128)(2,1)}, bf16[256,1024]{1,0:T(8,128)(2,1)S(1)}, u32[]{:S(2)}, u32[]{:S(2)}) collective-permute-start(bf16[256,1024]{1,0:T(8,128)(2,1)} %bitcast.16), channel_id=1, source_target_pairs={{0,480},{32,448},{64,416},{96,384},{128,352},{160,320},{192,288},{... | collective-permute-start | bytes 1572872 | tf_op jit(solution)/shard_map/ppermute | solution.py:240
  6.1 0.7 %convert_element_type.5 = f32[2048]{0:T(1024)S(1)} convert(s32[2048]{0:T(1024)} %param.9) | non-fusion elementwise | flops 2048 | bytes 16384 | tf_op jit(solution)/shard_map/convert_element_type | solution.py:241
  6.8 0.0 copy-start
  6.8 1.0 %copy-done = bf16[1,256,1024]{2,1,0:T(8,128)(2,1)S(1)} copy-done((bf16[1,256,1024]{2,1,0:T(8,128)(2,1)S(1)}, bf16[1,256,1024]{2,1,0:T(8,128)(2,1)}, u32[]{:S(2)}) %copy-start) | copy-done | bytes 524312
  7.9 0.0 copy-start.1
  7.9 0.8 %copy-done.1 = bf16[1,256,128]{2,1,0:T(8,128)(2,1)S(1)} copy-done((bf16[1,256,128]{2,1,0:T(8,128)(2,1)S(1)}, bf16[1,256,128]{2,1,0:T(8,128)(2,1)}, u32[]{:S(2)}) %copy-start.1) | copy-done | bytes 65560
  8.7 0.0 copy-start.2
  8.7 0.8 %copy-done.2 = bf16[1,256,128]{2,1,0:T(8,128)(2,1)S(1)} copy-done((bf16[1,256,128]{2,1,0:T(8,128)(2,1)S(1)}, bf16[1,256,128]{2,1,0:T(8,128)(2,1)}, u32[]{:S(2)}) %copy-start.2) | copy-done | bytes 65560
  9.6 22.8 %shard_map.84 = (bf16[256,1024]{1,0:T(8,128)(2,1)S(1)}, bf16[8,256,2048]{2,1,0:T(8,128)(2,1)}, bf16[8,256,128]{2,1,0:T(8,128)(2,1)S(1)}, bf16[8,256,128]{2,1,0:T(8,128)(2,1)S(1)}, f32[256,8]{1,0:T(8,128)S(1)}) custom-call(bf16[256,1024]{1,0:T(8,128)(2,1)S(1)} %bitcast.12, bf16[256,128]{1,0:T(8,128)(2,1)S(1)} %bitcast.14, bf16[256,128]{1,0:T(8,128)(2,1)S(1)} %bitcast.15, ...), custom_call_target="tpu_custom_call" | custom-call | flops 2147483648 | bytes 16777216 | tf_op jit(solution)/shard_map/pallas_call | solution.py:245
  32.3 0.0 collective-permute-done.cot_hbm
  32.3 29.1 %shard_map.85 = (bf16[256,1024]{1,0:T(8,128)(2,1)S(1)}, bf16[256,128]{1,0:T(8,128)(2,1)S(1)}, bf16[256,128]{1,0:T(8,128)(2,1)S(1)}) custom-call(bf16[256,1024]{1,0:T(8,128)(2,1)S(1)} %bitcast.13, bf16[256,1024]{1,0:T(8,128)(2,1)S(1)} %collective-permute-done.cot_hbm, bf16[8,256,2048]{2,1,0:T(8,128)(2,1)} %get-tuple-element.13.p_hbm, ...), custom_call_target="tpu_custom_call" | custom-call | flops 4294967296 | bytes 16777216 | tf_op jit(solution)/shard_map/pallas_call | solution.py:281
  61.5 0.8 %copy.13 = bf16[1,256,1024]{2,1,0:T(8,128)(2,1)} copy(bf16[1,256,1024]{2,1,0:T(8,128)(2,1)S(1)} %bitcast.8) | data formatting | bytes 1048576
  62.3 0.8 %copy.14 = bf16[1,256,1024]{2,1,0:T(8,128)(2,1)} copy(bf16[1,256,1024]{2,1,0:T(8,128)(2,1)S(1)} %bitcast.9) | data formatting | bytes 1048576
  63.1 0.6 copy.15
  63.7 0.6 copy.16
  (1 shorter events, 0.0 us)
Async XLA Ops:
  0.6 31.7 %collective-permute-start = (bf16[256,1024]{1,0:T(8,128)(2,1)}, bf16[256,1024]{1,0:T(8,128)(2,1)S(1)}, u32[]{:S(2)}, u32[]{:S(2)}) collective-permute-start(bf16[256,1024]{1,0:T(8,128)(2,1)} %bitcast.16), channel_id=1, source_target_pairs={{0,480},{32,448},{64,416},{96,384},{128,352},{160,320},{192,288},{... | collective-permute-start | bytes 1572872 | tf_op jit(solution)/shard_map/ppermute | solution.py:240
  6.8 1.0 %copy-start = (bf16[1,256,1024]{2,1,0:T(8,128)(2,1)S(1)}, bf16[1,256,1024]{2,1,0:T(8,128)(2,1)}, u32[]{:S(2)}) copy-start(bf16[1,256,1024]{2,1,0:T(8,128)(2,1)} %param.5) | copy-start | bytes 1572868
  7.9 0.8 %copy-start.1 = (bf16[1,256,128]{2,1,0:T(8,128)(2,1)S(1)}, bf16[1,256,128]{2,1,0:T(8,128)(2,1)}, u32[]{:S(2)}) copy-start(bf16[1,256,128]{2,1,0:T(8,128)(2,1)} %param.6) | copy-start | bytes 196612
  8.7 0.8 %copy-start.2 = (bf16[1,256,128]{2,1,0:T(8,128)(2,1)S(1)}, bf16[1,256,128]{2,1,0:T(8,128)(2,1)}, u32[]{:S(2)}) copy-start(bf16[1,256,128]{2,1,0:T(8,128)(2,1)} %param.7) | copy-start | bytes 196612

commit v2 on v1

v2 whole, which is shorter than its diff:
```python
import functools
import math

import jax
import jax.numpy as jnp
from jax import lax
from jax.experimental import pallas as pl
from jax.experimental.pallas import tpu as pltpu
from jax.sharding import PartitionSpec as P

HD = 128
MESH = pl.DeviceIdType.MESH
NT = (((1,), (1,)), ((), ()))
NN = (((1,), (0,)), ((), ()))
F32 = jnp.float32
BF16 = jnp.bfloat16
UNROLL = 8
SPREAD = 8
WEIGH = 1


def dot(a, b, dims):
    return lax.dot_general(a, b, dims, preferred_element_type=F32)


def place():
    return tuple(lax.axis_index(a) for a in ("section", "tensor", "seq"))


ORDER = ((1, 2), (0, 2), (1, 1), (1, 3), (0, 1), (0, 3), (1, 0), (0, 0))
OWN = 7


def peer(dz, dx):
    section, tensor, seq = place()
    z, x = seq // 4, seq % 4
    return (section, tensor, ((z + dz) % 2) * 4 + (x + dx) % 4)


def greet(devices):
    barrier = pltpu.get_barrier_semaphore()
    for device in devices:
        pl.semaphore_signal(barrier, inc=1, device_id=device, device_id_type=MESH)
    pl.semaphore_wait(barrier, len(devices))


def remote(src, dst, send, recv, device):
    return pltpu.make_async_remote_copy(
        src_ref=src, dst_ref=dst, send_sem=send, recv_sem=recv, device_id=device, device_id_type=MESH
    )


def each(count, body, unroll=1):
    if unroll >= count:
        for j in range(count):
            body(j)
        return

    def step(i, carry):
        for j in range(unroll):
            body(i * unroll + j)
        return carry

    lax.fori_loop(0, count // unroll, step, 0)


def block(index, size):
    return pl.ds(index * size if isinstance(index, int) else pl.multiple_of(index * size, size), size)


def fwd_kernel(
    heads, tok, q_hbm, k_hbm, v_hbm, pos_hbm, o_ref, probs, kbuf, vbuf, qst, inv_ref,
    pos, scores, bias, top, total, lsem, ksend, krecv, vsend, vrecv,
):
    loads = [
        pltpu.make_async_copy(q_hbm.at[:, pl.ds(h * HD, HD)], qst.at[pl.ds(h * tok, tok), :], lsem.at[h])
        for h in range(heads)
    ]
    loads.append(pltpu.make_async_copy(k_hbm, kbuf.at[OWN], lsem.at[heads]))
    loads.append(pltpu.make_async_copy(v_hbm, vbuf.at[OWN], lsem.at[heads + 1]))
    loads.append(pltpu.make_async_copy(pos_hbm, pos, lsem.at[heads + 2]))
    for c in loads:
        c.start()
    greet([peer(*ORDER[slot]) for slot in range(OWN)])
    sends = []
    for src, buf, send, recv in ((k_hbm, kbuf, ksend, krecv), (v_hbm, vbuf, vsend, vrecv)):
        for slot in range(OWN):
            dz, dx = ORDER[slot]
            back = ORDER.index((dz, (4 - dx) % 4))
            sends.append(remote(src, buf.at[back], send.at[slot], recv.at[back], peer(dz, dx)))
    for c in sends:
        c.start()
    for c in loads:
        c.wait()

    def pos_row(device):
        return pos[block(device, tok)].reshape(1, tok).astype(F32)

    rows = [pos_row(peer(dz, dx)[2]) for dz, dx in ORDER]
    k_cols = jnp.transpose(jnp.concatenate(rows, axis=0))
    for slot in range(8):
        bias[slot] = jnp.where(k_cols[:, slot : slot + 1] <= rows[OWN], 0.0, -1e30)
    top[...] = jnp.full_like(top, -1e30)
    total[...] = jnp.zeros_like(total)
    factor = HD**-0.5 * math.log2(math.e)

    def score(i):
        slot = OWN - i

        @pl.when(i > 0)
        def _():
            remote(kbuf.at[slot], kbuf.at[slot], ksend.at[slot], krecv.at[slot], peer(0, 1)).wait_recv()

        def one(h):
            columns = block(h, tok)
            part = dot(kbuf[slot], qst[columns, :], NT) * factor + bias[slot]
            scores[slot, :, columns] = part
            top[h] = jnp.maximum(top[h], jnp.max(part.reshape(tok // 8, 8, tok), axis=0))

        each(heads, one, UNROLL)

    each(8, score)

    def weigh(h):
        columns = block(h, tok)
        peak = jnp.max(top[h], axis=0, keepdims=True)

        def one(slot):
            raw = jnp.exp2(scores[slot, :, columns] - peak)
            total[h] += jnp.sum(raw.reshape(tok // 8, 8, tok), axis=0)
            probs[slot, :, columns] = raw.astype(BF16)

        each(8, one, UNROLL)

    each(heads, weigh, WEIGH)
    for slot in range(OWN):
        remote(vbuf.at[slot], vbuf.at[slot], vsend.at[slot], vrecv.at[slot], peer(0, 1)).wait_recv()
    vt = jnp.transpose(vbuf[...].reshape(8 * tok, HD))

    def mix(h):
        inv = jnp.broadcast_to(1.0 / jnp.sum(total[h], axis=0, keepdims=True), (HD, tok))
        mixed = dot(vt, probs[:, :, block(h, tok)].reshape(8 * tok, tok), NN)
        o_ref[:, block(h, HD)] = jnp.transpose(mixed * inv).astype(BF16)
        inv_ref[:, block(h, HD)] = jnp.transpose(inv)

    each(heads, mix, SPREAD)
    for c in sends:
        c.wait_send()


def bwd_kernel(
    heads, tok, cot_ref, probs, kbuf, vbuf, qst, o_ref, inv_ref, gq_ref, gk_ref, gv_ref,
    cst, dst, acc, dvec, sendbuf, far, near, across, ssem, rsem,
):
    scale = HD**-0.5
    right, left, over = peer(0, 1), peer(0, 3), peer(1, 0)
    greet([right, left, over])

    def prepare(h):
        columns = block(h, HD)
        cot = cot_ref[:, columns].astype(F32) * inv_ref[:, columns]
        drop = jnp.transpose(cot * o_ref[:, columns].astype(F32))
        dvec[pl.ds(h, 1), :] = jnp.sum(drop, axis=0, keepdims=True)
        cst[block(h, tok), :] = cot.astype(BF16)

    each(heads, prepare, SPREAD)

    def far_k(dz):
        return remote(sendbuf.at[1 - dz, 0], far.at[dz, 0], ssem.at[dz], rsem.at[dz], right)

    def far_v(dz):
        return remote(sendbuf.at[1 - dz, 1], far.at[dz, 1], ssem.at[2 + dz], rsem.at[2 + dz], left)

    def near_right(dz):
        return remote(sendbuf.at[4 - 2 * dz], near.at[dz, 0], ssem.at[4 + dz], rsem.at[4 + dz], right)

    def near_left(dz):
        return remote(sendbuf.at[5 - 2 * dz], near.at[dz, 1], ssem.at[6 + dz], rsem.at[6 + dz], left)

    def work(slot):
        def one(h):
            rows = block(h, tok)
            dp = dot(vbuf[slot], cst[rows, :], NT)
            part = probs[slot, :, rows].astype(F32) * (dp - dvec[pl.ds(h, 1), :])
            dst[slot, :, rows] = part.astype(BF16)

        each(heads, one, UNROLL)
        acc[0] = dot(dst[slot], qst[...], NN) * scale
        acc[1] = dot(probs[slot], cst[...], NN)

        @pl.when(slot < 2)
        def _():
            sendbuf[slot] = acc[0:2].astype(BF16)
            far_k(1 - slot).start()
            far_v(1 - slot).start()

        for dz in range(2):

            @pl.when(slot == 4 - 2 * dz)
            def _():
                far_k(dz).wait_recv()
                sendbuf[slot, 0] = (acc[0] + far[dz, 0].astype(F32)).astype(BF16)
                sendbuf[slot, 1] = acc[1].astype(BF16)
                near_right(dz).start()

            @pl.when(slot == 5 - 2 * dz)
            def _():
                far_v(dz).wait_recv()
                sendbuf[slot, 0] = acc[0].astype(BF16)
                sendbuf[slot, 1] = (acc[1] + far[dz, 1].astype(F32)).astype(BF16)
                near_left(dz).start()

        @pl.when(slot == 6)
        def _():
            acc[2:4] = acc[0:2]

    each(8, work)

    near_right(1).wait_recv()
    near_left(1).wait_recv()
    sendbuf[6] = (acc[2:4] + near[1, 0].astype(F32) + near[1, 1].astype(F32)).astype(BF16)
    cross = remote(sendbuf.at[6], across, ssem.at[8], rsem.at[8], over)
    cross.start()
    kt = jnp.transpose(kbuf[...].reshape(8 * tok, HD))

    def finish(h):
        part = dot(kt, dst[:, :, block(h, tok)].reshape(8 * tok, tok), NN) * scale
        gq_ref[:, block(h, HD)] = jnp.transpose(part).astype(BF16)

    each(heads, finish, SPREAD)
    near_right(0).wait_recv()
    near_left(0).wait_recv()
    cross.wait_recv()
    summed = acc[0:2] + near[0, 0].astype(F32) + near[0, 1].astype(F32) + across[...].astype(F32)
    gk_ref[...] = summed[0].astype(BF16)
    gv_ref[...] = summed[1].astype(BF16)
    cross.wait_send()
    for dz in range(2):
        for make in (far_k, far_v, near_right, near_left):
            make(dz).wait_send()


def local(queries, keys, values, cotangent, positions):
    q, k, v, cot = queries[0], keys[0], values[0], cotangent[0]
    tok, width = q.shape
    heads = width // HD
    wide = heads * tok
    count = lax.axis_size("section")
    mirrored = lax.ppermute(cot, "section", [(s, count - 1 - s) for s in range(count)])
    anywhere = pl.BlockSpec(memory_space=pl.ANY)
    vmem = pl.BlockSpec(memory_space=pltpu.VMEM)
    dma = pltpu.SemaphoreType.DMA
    out, probs, k_all, v_all, q_st, inverse = pl.pallas_call(
        functools.partial(fwd_kernel, heads, tok),
        out_shape=(
            jax.ShapeDtypeStruct((tok, width), BF16),
            jax.ShapeDtypeStruct((8, tok, wide), BF16),
            jax.ShapeDtypeStruct((8, tok, HD), BF16),
            jax.ShapeDtypeStruct((8, tok, HD), BF16),
            jax.ShapeDtypeStruct((wide, HD), BF16),
            jax.ShapeDtypeStruct((tok, width), F32),
        ),
        in_specs=[anywhere] * 4,
        out_specs=(vmem,) * 6,
        scratch_shapes=[
            pltpu.VMEM((8 * tok,), jnp.int32),
            pltpu.VMEM((8, tok, wide), F32),
            pltpu.VMEM((8, tok, tok), F32),
            pltpu.VMEM((heads, 8, tok), F32),
            pltpu.VMEM((heads, 8, tok), F32),
            dma((heads + 3,)),
            dma((8,)),
            dma((8,)),
            dma((8,)),
            dma((8,)),
        ],
        cost_estimate=pl.CostEstimate(
            flops=4 * wide * 8 * tok * HD, bytes_accessed=2**24, transcendentals=wide * 8 * tok
        ),
        compiler_params=pltpu.CompilerParams(
            collective_id=1, has_side_effects=True, vmem_limit_bytes=36 * 2**20
        ),
    )(q, k, v, positions)
    grad_q, grad_k, grad_v = pl.pallas_call(
        functools.partial(bwd_kernel, heads, tok),
        out_shape=(
            jax.ShapeDtypeStruct((tok, width), BF16),
            jax.ShapeDtypeStruct((tok, HD), BF16),
            jax.ShapeDtypeStruct((tok, HD), BF16),
        ),
        in_specs=[vmem] * 7,
        out_specs=(vmem,) * 3,
        scratch_shapes=[
            pltpu.VMEM((wide, HD), BF16),
            pltpu.VMEM((8, tok, wide), BF16),
            pltpu.VMEM((4, tok, HD), F32),
            pltpu.VMEM((heads, tok), F32),
            pltpu.VMEM((7, 2, tok, HD), BF16),
            pltpu.VMEM((2, 2, tok, HD), BF16),
            pltpu.VMEM((2, 2, 2, tok, HD), BF16),
            pltpu.VMEM((2, tok, HD), BF16),
            dma((9,)),
            dma((9,)),
        ],
        cost_estimate=pl.CostEstimate(
            flops=8 * wide * 8 * tok * HD, bytes_accessed=2**24, transcendentals=0
        ),
        compiler_params=pltpu.CompilerParams(
            collective_id=2, has_side_effects=True, vmem_limit_bytes=36 * 2**20
        ),
    )(mirrored, probs, k_all, v_all, q_st, out, inverse)
    return (out[None], grad_q[None], grad_k[None], grad_v[None])


def solution(mesh):
    split = P("section", "seq", "tensor")
    return jax.shard_map(
        local,
        mesh=mesh,
        in_specs=(split, split, split, split, P()),
        out_specs=(split, split, split, split),
        check_vma=False,
    )
```

time: 64.7 us -> 53.2 us (0.82)
  the two profiles are of different devices: /device:TPU:14 before, /device:TPU:160 now
where the time goes in v2:
time: 53.2 us; the launch traced here: 52.8 us
  Pallas kernels  42 us (79%)
  local copies, waits for them, and re-layouts  6.26 us (12%)
  waiting for transfers between devices  1.99 us (4%)
  starting transfers between devices  1.92 us (4%)
  between operations  0.67 us (1%)
    pallas_call x1, Pallas kernels, local(): pl.pallas_call(functools.partial(fwd_kernel, heads, tok), out_shape=(jax....  21.4 us
    pallas_call x1, Pallas kernels, local(): pl.pallas_call(functools.partial(bwd_kernel, heads, tok), out_shape=(jax....  20.5 us
    unnamed x12, local copies, waits for them, and re-layouts  6.26 us
    ppermute x1, waiting for transfers between devices, local(): lax.ppermute(cot, 'section', [(s, count - 1 - s) for s in range(count)])  1.99 us
    ppermute x1, starting transfers between devices, local(): lax.ppermute(cot, 'section', [(s, count - 1 - s) for s in range(count)])  1.92 us
  transfers between devices with their start and end apart: 1, of which 1 were waited for; matrix products, arithmetic and copies ran while one was open for 0% of the time, Pallas kernels for 41%

profile of v2, /device:TPU:160, one launch (start us, length us, event | category | flops | bytes accessed | tf_op | source)
XLA Modules:
  0.0 52.8 jit_solution(12353889313798651382)
XLA Ops:
  0.6 1.9 %collective-permute-start = (bf16[256,1024]{1,0:T(8,128)(2,1)}, bf16[256,1024]{1,0:T(8,128)(2,1)S(1)}, u32[]{:S(2)}, u32[]{:S(2)}) collective-permute-start(bf16[256,1024]{1,0:T(8,128)(2,1)} %bitcast.15), channel_id=1, source_target_pairs={{0,480},{32,448},{64,416},{96,384},{128,352},{160,320},{192,288},{... | collective-permute-start | bytes 1572872 | tf_op jit(solution)/shard_map/ppermute | solution.py:249
  2.6 0.0 copy-start
  2.6 1.0 %copy-done = bf16[1,256,1024]{2,1,0:T(8,128)(2,1)S(1)} copy-done((bf16[1,256,1024]{2,1,0:T(8,128)(2,1)S(1)}, bf16[1,256,1024]{2,1,0:T(8,128)(2,1)}, u32[]{:S(2)}) %copy-start) | copy-done | bytes 524312
  3.6 0.0 copy-start.1
  3.6 0.8 %copy-done.1 = bf16[1,256,128]{2,1,0:T(8,128)(2,1)S(1)} copy-done((bf16[1,256,128]{2,1,0:T(8,128)(2,1)S(1)}, bf16[1,256,128]{2,1,0:T(8,128)(2,1)}, u32[]{:S(2)}) %copy-start.1) | copy-done | bytes 65560
  4.4 0.0 copy-start.2
  4.4 0.8 %copy-done.2 = bf16[1,256,128]{2,1,0:T(8,128)(2,1)S(1)} copy-done((bf16[1,256,128]{2,1,0:T(8,128)(2,1)S(1)}, bf16[1,256,128]{2,1,0:T(8,128)(2,1)}, u32[]{:S(2)}) %copy-start.2) | copy-done | bytes 65560
  5.3 0.0 copy-start.3
  5.3 0.7 %copy-done.3 = s32[2048]{0:T(1024)S(1)} copy-done((s32[2048]{0:T(1024)S(1)}, s32[2048]{0:T(1024)}, u32[]{:S(2)}) %copy-start.3) | copy-done | bytes 8216
  6.0 21.4 %shard_map.84 = (bf16[256,1024]{1,0:T(8,128)(2,1)S(1)}, bf16[8,256,2048]{2,1,0:T(8,128)(2,1)S(1)}, bf16[8,256,128]{2,1,0:T(8,128)(2,1)S(1)}, bf16[8,256,128]{2,1...) custom-call(bf16[256,1024]{1,0:T(8,128)(2,1)S(1)} %bitcast.12, ...), custom_call_target="tpu_custom_call" | custom-call | flops 2147483648 | bytes 16777216 | tf_op jit(solution)/shard_map/pallas_call | solution.py:253
  27.4 2.0 %collective-permute-done.cot_ref = bf16[256,1024]{1,0:T(8,128)(2,1)S(1)} collective-permute-done((bf16[256,1024]{1,0:T(8,128)(2,1)}, bf16[256,1024]{1,0:T(8,128)(2,1)S(1)}, u32[]{:S(2)}, u32[]{:S(2)}) %collective-permute-start) | collective-permute-done | bytes 524320 | tf_op jit(solution)/shard_map/ppermute | solution.py:249
  29.4 20.5 %shard_map.85 = (bf16[256,1024]{1,0:T(8,128)(2,1)S(1)}, bf16[256,128]{1,0:T(8,128)(2,1)S(1)}, bf16[256,128]{1,0:T(8,128)(2,1)S(1)}) custom-call(bf16[256,1024]{1,0:T(8,128)(2,1)S(1)} %collective-permute-done.cot_ref, bf16[8,256,2048]{2,1,0:T(8,128)(2,1)S(1)} %get-tuple-element.14.probs, bf16[8,256,128]{2,1,0:T(8,128)(2,1)S(1)} %get-tuple-element.15.kbuf, ...), custom_call_target="tpu_custom_call" | custom-call | flops 4294967296 | bytes 16777216 | tf_op jit(solution)/shard_map/pallas_call | solution.py:284
  49.9 0.8 %copy.13 = bf16[1,256,1024]{2,1,0:T(8,128)(2,1)} copy(bf16[1,256,1024]{2,1,0:T(8,128)(2,1)S(1)} %bitcast.8) | data formatting | bytes 1048576
  50.7 0.8 %copy.14 = bf16[1,256,1024]{2,1,0:T(8,128)(2,1)} copy(bf16[1,256,1024]{2,1,0:T(8,128)(2,1)S(1)} %bitcast.9) | data formatting | bytes 1048576
  51.5 0.6 %copy.15 = bf16[1,256,128]{2,1,0:T(8,128)(2,1)} copy(bf16[1,256,128]{2,1,0:T(8,128)(2,1)S(1)} %bitcast.11) | data formatting | bytes 131072
  52.2 0.6 %copy.16 = bf16[1,256,128]{2,1,0:T(8,128)(2,1)} copy(bf16[1,256,128]{2,1,0:T(8,128)(2,1)S(1)} %bitcast.10) | data formatting | bytes 131072
Async XLA Ops:
  0.6 28.8 %collective-permute-start = (bf16[256,1024]{1,0:T(8,128)(2,1)}, bf16[256,1024]{1,0:T(8,128)(2,1)S(1)}, u32[]{:S(2)}, u32[]{:S(2)}) collective-permute-start(bf16[256,1024]{1,0:T(8,128)(2,1)} %bitcast.15), channel_id=1, source_target_pairs={{0,480},{32,448},{64,416},{96,384},{128,352},{160,320},{192,288},{... | collective-permute-start | bytes 1572872 | tf_op jit(solution)/shard_map/ppermute | solution.py:249
  2.6 1.0 %copy-start = (bf16[1,256,1024]{2,1,0:T(8,128)(2,1)S(1)}, bf16[1,256,1024]{2,1,0:T(8,128)(2,1)}, u32[]{:S(2)}) copy-start(bf16[1,256,1024]{2,1,0:T(8,128)(2,1)} %param.5) | copy-start | bytes 1572868
  3.6 0.8 %copy-start.1 = (bf16[1,256,128]{2,1,0:T(8,128)(2,1)S(1)}, bf16[1,256,128]{2,1,0:T(8,128)(2,1)}, u32[]{:S(2)}) copy-start(bf16[1,256,128]{2,1,0:T(8,128)(2,1)} %param.6) | copy-start | bytes 196612
  4.4 0.8 %copy-start.2 = (bf16[1,256,128]{2,1,0:T(8,128)(2,1)S(1)}, bf16[1,256,128]{2,1,0:T(8,128)(2,1)}, u32[]{:S(2)}) copy-start(bf16[1,256,128]{2,1,0:T(8,128)(2,1)} %param.7) | copy-start | bytes 196612
  5.3 0.7 %copy-start.3 = (s32[2048]{0:T(1024)S(1)}, s32[2048]{0:T(1024)}, u32[]{:S(2)}) copy-start(s32[2048]{0:T(1024)} %pos_hbm.1) | copy-start | bytes 24580

commit v3 on v2

--- a/solution.py
+++ b/solution.py
@@ -27,7 +27,7 @@
     return tuple(lax.axis_index(a) for a in ("section", "tensor", "seq"))
 
 
-ORDER = ((1, 2), (0, 2), (1, 1), (1, 3), (0, 1), (0, 3), (1, 0), (0, 0))
+ORDER = ((1, 2), (1, 1), (1, 3), (0, 2), (1, 0), (0, 1), (0, 3), (0, 0))
 OWN = 7
 
 
@@ -150,7 +150,7 @@
 
 def bwd_kernel(
     heads, tok, cot_ref, probs, kbuf, vbuf, qst, o_ref, inv_ref, gq_ref, gk_ref, gv_ref,
-    cst, dst, acc, dvec, sendbuf, far, near, across, ssem, rsem,
+    cst, dst, acc, hold, dvec, sendbuf, zin, far1, far0, near1, near0, across, ssem, rsem,
 ):
     scale = HD**-0.5
     right, left, over = peer(0, 1), peer(0, 3), peer(1, 0)
@@ -165,17 +165,20 @@
 
     each(heads, prepare, SPREAD)
 
-    def far_k(dz):
-        return remote(sendbuf.at[1 - dz, 0], far.at[dz, 0], ssem.at[dz], rsem.at[dz], right)
-
-    def far_v(dz):
-        return remote(sendbuf.at[1 - dz, 1], far.at[dz, 1], ssem.at[2 + dz], rsem.at[2 + dz], left)
-
-    def near_right(dz):
-        return remote(sendbuf.at[4 - 2 * dz], near.at[dz, 0], ssem.at[4 + dz], rsem.at[4 + dz], right)
-
-    def near_left(dz):
-        return remote(sendbuf.at[5 - 2 * dz], near.at[dz, 1], ssem.at[6 + dz], rsem.at[6 + dz], left)
+    def hop(number, src, dst_ref, device):
+        return remote(src, dst_ref, ssem.at[number], rsem.at[number], device)
+
+    top, low = pl.ds(0, tok // 2), pl.ds(tok // 2, tok // 2)
+    pair = {dx: hop(dx, sendbuf.at[ORDER.index((1, dx)), 1], zin.at[dx], over) for dx in range(4)}
+    far1_right = hop(4, sendbuf.at[0, 0, top], far1.at[0], right)
+    far1_left = hop(5, sendbuf.at[0, 0, low], far1.at[1], left)
+    far0_right = hop(6, sendbuf.at[3, 0], far0.at[0], right)
+    far0_left = hop(7, sendbuf.at[3, 1], far0.at[1], left)
+    near1_right = hop(8, sendbuf.at[1, 0], near1.at[0], right)
+    near1_left = hop(9, sendbuf.at[2, 0], near1.at[1], left)
+    near0_right = hop(10, sendbuf.at[5], near0.at[0], right)
+    near0_left = hop(11, sendbuf.at[6], near0.at[1], left)
+    cross = hop(12, sendbuf.at[4, 0], across, over)
 
     def work(slot):
         def one(h):
@@ -188,39 +191,68 @@
         acc[0] = dot(dst[slot], qst[...], NN) * scale
         acc[1] = dot(probs[slot], cst[...], NN)
 
-        @pl.when(slot < 2)
-        def _():
-            sendbuf[slot] = acc[0:2].astype(BF16)
-            far_k(1 - slot).start()
-            far_v(1 - slot).start()
-
-        for dz in range(2):
-
-            @pl.when(slot == 4 - 2 * dz)
-            def _():
-                far_k(dz).wait_recv()
-                sendbuf[slot, 0] = (acc[0] + far[dz, 0].astype(F32)).astype(BF16)
-                sendbuf[slot, 1] = acc[1].astype(BF16)
-                near_right(dz).start()
-
-            @pl.when(slot == 5 - 2 * dz)
-            def _():
-                far_v(dz).wait_recv()
-                sendbuf[slot, 0] = acc[0].astype(BF16)
-                sendbuf[slot, 1] = (acc[1] + far[dz, 1].astype(F32)).astype(BF16)
-                near_left(dz).start()
+        @pl.when(slot == 0)
+        def _():
+            sendbuf[0] = acc[...].astype(BF16)
+            far1_right.start()
+            far1_left.start()
+            pair[2].start()
+
+        @pl.when(slot == 1)
+        def _():
+            sendbuf[1, 1] = acc[1].astype(BF16)
+            pair[1].start()
+            hold[0] = acc[0]
+
+        @pl.when(slot == 2)
+        def _():
+            sendbuf[2, 1] = acc[1].astype(BF16)
+            pair[3].start()
+            far1_right.wait_recv()
+            sendbuf[1, 0, top] = (hold[0, top] + far1[0].astype(F32)).astype(BF16)
+            sendbuf[1, 0, low] = hold[0, low].astype(BF16)
+            near1_right.start()
+            far1_left.wait_recv()
+            sendbuf[2, 0, top] = acc[0, top].astype(BF16)
+            sendbuf[2, 0, low] = (acc[0, low] + far1[1].astype(F32)).astype(BF16)
+            near1_left.start()
+
+        @pl.when(slot == 3)
+        def _():
+            sendbuf[3, 0] = acc[0].astype(BF16)
+            far0_right.start()
+            pair[2].wait_recv()
+            sendbuf[3, 1] = (acc[1] + zin[2].astype(F32)).astype(BF16)
+            far0_left.start()
+
+        @pl.when(slot == 4)
+        def _():
+            sendbuf[4, 1] = acc[1].astype(BF16)
+            pair[0].start()
+            hold[1] = acc[0]
+
+        @pl.when(slot == 5)
+        def _():
+            hold[2:4] = acc[...]
 
         @pl.when(slot == 6)
         def _():
-            acc[2:4] = acc[0:2]
+            far0_right.wait_recv()
+            pair[1].wait_recv()
+            sendbuf[5, 0] = (hold[2] + far0[0].astype(F32)).astype(BF16)
+            sendbuf[5, 1] = (hold[3] + zin[1].astype(F32)).astype(BF16)
+            near0_right.start()
+            far0_left.wait_recv()
+            pair[3].wait_recv()
+            sendbuf[6, 0] = acc[0].astype(BF16)
+            sendbuf[6, 1] = (acc[1] + zin[3].astype(F32) + far0[1].astype(F32)).astype(BF16)
+            near0_left.start()
+            near1_right.wait_recv()
+            near1_left.wait_recv()
+            sendbuf[4, 0] = (hold[1] + near1[0].astype(F32) + near1[1].astype(F32)).astype(BF16)
+            cross.start()
 
     each(8, work)
-
-    near_right(1).wait_recv()
-    near_left(1).wait_recv()
-    sendbuf[6] = (acc[2:4] + near[1, 0].astype(F32) + near[1, 1].astype(F32)).astype(BF16)
-    cross = remote(sendbuf.at[6], across, ssem.at[8], rsem.at[8], over)
-    cross.start()
     kt = jnp.transpose(kbuf[...].reshape(8 * tok, HD))
 
     def finish(h):
@@ -228,20 +260,27 @@
         gq_ref[:, block(h, HD)] = jnp.transpose(part).astype(BF16)
 
     each(heads, finish, SPREAD)
-    near_right(0).wait_recv()
-    near_left(0).wait_recv()
+    pair[0].wait_recv()
+    gv = acc[1] + zin[0].astype(F32)
+    gk = acc[0]
+    near0_right.wait_recv()
+    near0_left.wait_recv()
     cross.wait_recv()
-    summed = acc[0:2] + near[0, 0].astype(F32) + near[0, 1].astype(F32) + across[...].astype(F32)
-    gk_ref[...] = summed[0].astype(BF16)
-    gv_ref[...] = summed[1].astype(BF16)
-    cross.wait_send()
-    for dz in range(2):
-        for make in (far_k, far_v, near_right, near_left):
-            make(dz).wait_send()
+    gk_ref[...] = (
+        gk + near0[0, 0].astype(F32) + near0[1, 0].astype(F32) + across[...].astype(F32)
+    ).astype(BF16)
+    gv_ref[...] = (gv + near0[0, 1].astype(F32) + near0[1, 1].astype(F32)).astype(BF16)
+    for c in (*pair.values(), far1_right, far1_left, far0_right, far0_left):
+        c.wait_send()
+    for c in (near1_right, near1_left, near0_right, near0_left, cross):
+        c.wait_send()
 
 
 def local(queries, keys, values, cotangent, positions):
     q, k, v, cot = queries[0], keys[0], values[0], cotangent[0]
+    q, k, v, positions = (
+        pltpu.with_memory_space_constraint(a, pltpu.HBM) for a in (q, k, v, positions)
+    )
     tok, width = q.shape
     heads = width // HD
     wide = heads * tok
@@ -293,14 +332,18 @@
         scratch_shapes=[
             pltpu.VMEM((wide, HD), BF16),
             pltpu.VMEM((8, tok, wide), BF16),
+            pltpu.VMEM((2, tok, HD), F32),
             pltpu.VMEM((4, tok, HD), F32),
             pltpu.VMEM((heads, tok), F32),
             pltpu.VMEM((7, 2, tok, HD), BF16),
+            pltpu.VMEM((4, tok, HD), BF16),
+            pltpu.VMEM((2, tok // 2, HD), BF16),
+            pltpu.VMEM((2, tok, HD), BF16),
+            pltpu.VMEM((2, tok, HD), BF16),
             pltpu.VMEM((2, 2, tok, HD), BF16),
-            pltpu.VMEM((2, 2, 2, tok, HD), BF16),
-            pltpu.VMEM((2, tok, HD), BF16),
-            dma((9,)),
-            dma((9,)),
+            pltpu.VMEM((tok, HD), BF16),
+            dma((13,)),
+            dma((13,)),
         ],
         cost_estimate=pl.CostEstimate(
             flops=8 * wide * 8 * tok * HD, bytes_accessed=2**24, transcendentals=0

time: 53.2 us -> 50.7 us (0.953)
  waiting for transfers between devices: 1.99 us -> 5.62 us
  local copies, waits for them, and re-layouts: 6.26 us -> 2.85 us
  Pallas kernels: 42 us -> 39.5 us
    ppermute x1, waiting for transfers between devices: 1.99 us -> 5.62 us  [local(): lax.ppermute(cot, 'section', [(s, count - 1 - s) for s in range(count)])]
    unnamed x12 -> x4, local copies, waits for them, and re-layouts: 6.26 us -> 2.85 us
    pallas_call x1, Pallas kernels: 20.5 us -> 18.2 us  [local(): pl.pallas_call(functools.partial(bwd_kernel, heads, tok), out_shape=(jax....]
  transfers between devices with their start and end apart: 1 -> 1, of which waited for: 1 -> 1; matrix products, arithmetic and copies ran while one was open for 0% -> 0% of each run, Pallas kernels for 41% -> 42%
where the time goes in v3:
time: 50.7 us; the launch traced here: 50.5 us
  Pallas kernels  39.5 us (78%)
  waiting for transfers between devices  5.62 us (11%)
  local copies, waits for them, and re-layouts  2.85 us (6%)
  starting transfers between devices  1.92 us (4%)
  between operations  0.66 us (1%)
    pallas_call x1, Pallas kernels, local(): pl.pallas_call(functools.partial(fwd_kernel, heads, tok), out_shape=(jax....  21.2 us
    pallas_call x1, Pallas kernels, local(): pl.pallas_call(functools.partial(bwd_kernel, heads, tok), out_shape=(jax....  18.2 us
    ppermute x1, waiting for transfers between devices, local(): lax.ppermute(cot, 'section', [(s, count - 1 - s) for s in range(count)])  5.62 us
    unnamed x4, local copies, waits for them, and re-layouts  2.85 us
    ppermute x1, starting transfers between devices, local(): lax.ppermute(cot, 'section', [(s, count - 1 - s) for s in range(count)])  1.92 us
  transfers between devices with their start and end apart: 1, of which 1 were waited for; matrix products, arithmetic and copies ran while one was open for 0% of the time, Pallas kernels for 42%

profile of v3, /device:TPU:160, one launch (start us, length us, event | category | flops | bytes accessed | tf_op | source)
XLA Modules:
  0.0 50.5 jit_solution(13744657960195635644)
XLA Ops:
  0.6 1.9 %collective-permute-start = (bf16[256,1024]{1,0:T(8,128)(2,1)}, bf16[256,1024]{1,0:T(8,128)(2,1)S(1)}, u32[]{:S(2)}, u32[]{:S(2)}) collective-permute-start(bf16[256,1024]{1,0:T(8,128)(2,1)} %bitcast.13), channel_id=1, source_target_pairs={{0,480},{32,448},{64,416},{96,384},{128,352},{160,320},{192,288},{... | collective-permute-start | bytes 1572872 | tf_op jit(solution)/shard_map/ppermute | solution.py:288
  2.6 21.2 %shard_map.84 = (bf16[256,1024]{1,0:T(8,128)(2,1)S(1)}, bf16[8,256,2048]{2,1,0:T(8,128)(2,1)S(1)}, bf16[8,256,128]{2,1,0:T(8,128)(2,1)S(1)}, bf16[8,256,128]{2,1...) custom-call(bf16[256,1024]{1,0:T(8,128)(2,1)} %bitcast.12, bf16[256,128]{1,0:T(8,128)(2,1)} %bitcast.14, ...), custom_call_target="tpu_custom_call" | custom-call | flops 2147483648 | bytes 16777216 | tf_op jit(solution)/shard_map/pallas_call | solution.py:292
  23.8 5.6 %collective-permute-done.cot_ref = bf16[256,1024]{1,0:T(8,128)(2,1)S(1)} collective-permute-done((bf16[256,1024]{1,0:T(8,128)(2,1)}, bf16[256,1024]{1,0:T(8,128)(2,1)S(1)}, u32[]{:S(2)}, u32[]{:S(2)}) %collective-permute-start) | collective-permute-done | bytes 524320 | tf_op jit(solution)/shard_map/ppermute | solution.py:288
  29.4 18.2 %shard_map.85 = (bf16[256,1024]{1,0:T(8,128)(2,1)S(1)}, bf16[256,128]{1,0:T(8,128)(2,1)S(1)}, bf16[256,128]{1,0:T(8,128)(2,1)S(1)}) custom-call(bf16[256,1024]{1,0:T(8,128)(2,1)S(1)} %collective-permute-done.cot_ref, bf16[8,256,2048]{2,1,0:T(8,128)(2,1)S(1)} %get-tuple-element.14.probs, bf16[8,256,128]{2,1,0:T(8,128)(2,1)S(1)} %get-tuple-element.15.kbuf, ...), custom_call_target="tpu_custom_call" | custom-call | flops 4294967296 | bytes 16777216 | tf_op jit(solution)/shard_map/pallas_call | solution.py:323
  47.6 0.8 %copy.13 = bf16[1,256,1024]{2,1,0:T(8,128)(2,1)} copy(bf16[1,256,1024]{2,1,0:T(8,128)(2,1)S(1)} %bitcast.8) | data formatting | bytes 1048576
  48.4 0.8 %copy.14 = bf16[1,256,1024]{2,1,0:T(8,128)(2,1)} copy(bf16[1,256,1024]{2,1,0:T(8,128)(2,1)S(1)} %bitcast.9) | data formatting | bytes 1048576
  49.2 0.6 %copy.15 = bf16[1,256,128]{2,1,0:T(8,128)(2,1)} copy(bf16[1,256,128]{2,1,0:T(8,128)(2,1)S(1)} %bitcast.11) | data formatting | bytes 131072
  49.9 0.6 %copy.16 = bf16[1,256,128]{2,1,0:T(8,128)(2,1)} copy(bf16[1,256,128]{2,1,0:T(8,128)(2,1)S(1)} %bitcast.10) | data formatting | bytes 131072
Async XLA Ops:
  0.6 28.8 %collective-permute-start = (bf16[256,1024]{1,0:T(8,128)(2,1)}, bf16[256,1024]{1,0:T(8,128)(2,1)S(1)}, u32[]{:S(2)}, u32[]{:S(2)}) collective-permute-start(bf16[256,1024]{1,0:T(8,128)(2,1)} %bitcast.13), channel_id=1, source_target_pairs={{0,480},{32,448},{64,416},{96,384},{128,352},{160,320},{192,288},{... | collective-permute-start | bytes 1572872 | tf_op jit(solution)/shard_map/ppermute | solution.py:288

commit v4 on v3

--- a/solution.py
+++ b/solution.py
@@ -149,7 +149,7 @@
 
 
 def bwd_kernel(
-    heads, tok, cot_ref, probs, kbuf, vbuf, qst, o_ref, inv_ref, gq_ref, gk_ref, gv_ref,
+    heads, tok, cot_ref, probs, kbuf, vbuf, qst, o_ref, inv_ref, done_ref, gq_ref, gk_ref, gv_ref,
     cst, dst, acc, hold, dvec, sendbuf, zin, far1, far0, near1, near0, across, ssem, rsem,
 ):
     scale = HD**-0.5
@@ -176,9 +176,9 @@
     far0_left = hop(7, sendbuf.at[3, 1], far0.at[1], left)
     near1_right = hop(8, sendbuf.at[1, 0], near1.at[0], right)
     near1_left = hop(9, sendbuf.at[2, 0], near1.at[1], left)
-    near0_right = hop(10, sendbuf.at[5], near0.at[0], right)
-    near0_left = hop(11, sendbuf.at[6], near0.at[1], left)
-    cross = hop(12, sendbuf.at[4, 0], across, over)
+    near0_right = [hop(10 + i, sendbuf.at[5, i], near0.at[0, i], right) for i in range(2)]
+    near0_left = [hop(12 + i, sendbuf.at[6, i], near0.at[1, i], left) for i in range(2)]
+    cross = hop(14, sendbuf.at[4, 0], across, over)
 
     def work(slot):
         def one(h):
@@ -233,26 +233,28 @@
 
         @pl.when(slot == 5)
         def _():
-            hold[2:4] = acc[...]
+            hold[2] = acc[0]
+            pair[1].wait_recv()
+            sendbuf[5, 1] = (acc[1] + zin[1].astype(F32)).astype(BF16)
+            near0_right[1].start()
 
         @pl.when(slot == 6)
         def _():
+            sendbuf[6, 0] = acc[0].astype(BF16)
+            near0_left[0].start()
             far0_right.wait_recv()
-            pair[1].wait_recv()
             sendbuf[5, 0] = (hold[2] + far0[0].astype(F32)).astype(BF16)
-            sendbuf[5, 1] = (hold[3] + zin[1].astype(F32)).astype(BF16)
-            near0_right.start()
+            near0_right[0].start()
+            pair[3].wait_recv()
             far0_left.wait_recv()
-            pair[3].wait_recv()
-            sendbuf[6, 0] = acc[0].astype(BF16)
             sendbuf[6, 1] = (acc[1] + zin[3].astype(F32) + far0[1].astype(F32)).astype(BF16)
-            near0_left.start()
+            near0_left[1].start()
             near1_right.wait_recv()
             near1_left.wait_recv()
             sendbuf[4, 0] = (hold[1] + near1[0].astype(F32) + near1[1].astype(F32)).astype(BF16)
             cross.start()
 
-    each(8, work)
+    each(8, work, 8)
     kt = jnp.transpose(kbuf[...].reshape(8 * tok, HD))
 
     def finish(h):
@@ -263,17 +265,23 @@
     pair[0].wait_recv()
     gv = acc[1] + zin[0].astype(F32)
     gk = acc[0]
-    near0_right.wait_recv()
-    near0_left.wait_recv()
-    cross.wait_recv()
+    for c in (*near0_right, *near0_left, cross):
+        c.wait_recv()
     gk_ref[...] = (
         gk + near0[0, 0].astype(F32) + near0[1, 0].astype(F32) + across[...].astype(F32)
     ).astype(BF16)
     gv_ref[...] = (gv + near0[0, 1].astype(F32) + near0[1, 1].astype(F32)).astype(BF16)
     for c in (*pair.values(), far1_right, far1_left, far0_right, far0_left):
         c.wait_send()
-    for c in (near1_right, near1_left, near0_right, near0_left, cross):
+    for c in (near1_right, near1_left, *near0_right, *near0_left, cross):
         c.wait_send()
+
+
+def keep_kernel(o_ref, o_hbm, done_ref, sem):
+    copy = pltpu.make_async_copy(o_ref, o_hbm, sem)
+    copy.start()
+    done_ref[...] = jnp.zeros_like(done_ref)
+    copy.wait()
 
 
 def local(queries, keys, values, cotangent, positions):
@@ -320,6 +328,14 @@
             collective_id=1, has_side_effects=True, vmem_limit_bytes=36 * 2**20
         ),
     )(q, k, v, positions)
+    kept, done = pl.pallas_call(
+        keep_kernel,
+        out_shape=(jax.ShapeDtypeStruct((tok, width), BF16), jax.ShapeDtypeStruct((8, HD), F32)),
+        in_specs=[vmem],
+        out_specs=(pl.BlockSpec(memory_space=pltpu.HBM), vmem),
+        scratch_shapes=[dma],
+        compiler_params=pltpu.CompilerParams(vmem_limit_bytes=2**20),
+    )(out)
     grad_q, grad_k, grad_v = pl.pallas_call(
         functools.partial(bwd_kernel, heads, tok),
         out_shape=(
@@ -327,13 +343,13 @@
             jax.ShapeDtypeStruct((tok, HD), BF16),
             jax.ShapeDtypeStruct((tok, HD), BF16),
         ),
-        in_specs=[vmem] * 7,
+        in_specs=[vmem] * 8,
         out_specs=(vmem,) * 3,
         scratch_shapes=[
             pltpu.VMEM((wide, HD), BF16),
             pltpu.VMEM((8, tok, wide), BF16),
             pltpu.VMEM((2, tok, HD), F32),
-            pltpu.VMEM((4, tok, HD), F32),
+            pltpu.VMEM((3, tok, HD), F32),
             pltpu.VMEM((heads, tok), F32),
             pltpu.VMEM((7, 2, tok, HD), BF16),
             pltpu.VMEM((4, tok, HD), BF16),
@@ -342,8 +358,8 @@
             pltpu.VMEM((2, tok, HD), BF16),
             pltpu.VMEM((2, 2, tok, HD), BF16),
             pltpu.VMEM((tok, HD), BF16),
-            dma((13,)),
-            dma((13,)),
+            dma((15,)),
+            dma((15,)),
         ],
         cost_estimate=pl.CostEstimate(
             flops=8 * wide * 8 * tok * HD, bytes_accessed=2**24, transcendentals=0
@@ -351,8 +367,8 @@
         compiler_params=pltpu.CompilerParams(
             collective_id=2, has_side_effects=True, vmem_limit_bytes=36 * 2**20
         ),
-    )(mirrored, probs, k_all, v_all, q_st, out, inverse)
-    return (out[None], grad_q[None], grad_k[None], grad_v[None])
+    )(mirrored, probs, k_all, v_all, q_st, out, inverse, done)
+    return (kept[None], grad_q[None], grad_k[None], grad_v[None])
 
 
 def solution(mesh):

time: 50.7 us -> 50 us (0.986)
  Pallas kernels: 39.5 us -> 40.4 us
  waiting for transfers between devices: 5.62 us -> 4.81 us
  local copies, waits for them, and re-layouts: 2.85 us -> 2.05 us
    ppermute x1, waiting for transfers between devices: 5.62 us -> 4.81 us  [local(): lax.ppermute(cot, 'section', [(s, count - 1 - s) for s in range(count)])]
    pallas_call x0 -> x1, Pallas kernels: none -> 0.8 us  [local(): pl.pallas_call(keep_kernel, out_shape=(jax.ShapeDtypeStruct((tok, width),...]
    unnamed x4 -> x3, local copies, waits for them, and re-layouts: 2.85 us -> 2.05 us
  transfers between devices with their start and end apart: 1 -> 1, of which waited for: 1 -> 1; matrix products, arithmetic and copies ran while one was open for 0% -> 0% of each run, Pallas kernels for 42% -> 44%
where the time goes in v4:
time: 50 us; the launch traced here: 49.8 us
  Pallas kernels  40.4 us (81%)
  waiting for transfers between devices  4.81 us (10%)
  local copies, waits for them, and re-layouts  2.05 us (4%)
  starting transfers between devices  1.92 us (4%)
  between operations  0.67 us (1%)
    pallas_call x1, Pallas kernels, local(): pl.pallas_call(functools.partial(fwd_kernel, heads, tok), out_shape=(jax....  21.2 us
    pallas_call x1, Pallas kernels, local(): pl.pallas_call(functools.partial(bwd_kernel, heads, tok), out_shape=(jax....  18.4 us
    ppermute x1, waiting for transfers between devices, local(): lax.ppermute(cot, 'section', [(s, count - 1 - s) for s in range(count)])  4.81 us
    unnamed x3, local copies, waits for them, and re-layouts  2.05 us
    ppermute x1, starting transfers between devices, local(): lax.ppermute(cot, 'section', [(s, count - 1 - s) for s in range(count)])  1.92 us
  transfers between devices with their start and end apart: 1, of which 1 were waited for; matrix products, arithmetic and copies ran while one was open for 0% of the time, Pallas kernels for 44%

profile of v4, /device:TPU:160, one launch (start us, length us, event | category | flops | bytes accessed | tf_op | source)
XLA Modules:
  0.0 49.8 jit_solution(15914070488719617380)
XLA Ops:
  0.6 1.9 %collective-permute-start = (bf16[256,1024]{1,0:T(8,128)(2,1)}, bf16[256,1024]{1,0:T(8,128)(2,1)S(1)}, u32[]{:S(2)}, u32[]{:S(2)}) collective-permute-start(bf16[256,1024]{1,0:T(8,128)(2,1)} %bitcast.12), channel_id=1, source_target_pairs={{0,480},{32,448},{64,416},{96,384},{128,352},{160,320},{192,288},{... | collective-permute-start | bytes 1572872 | tf_op jit(solution)/shard_map/ppermute | solution.py:296
  2.6 21.2 %shard_map.84 = (bf16[256,1024]{1,0:T(8,128)(2,1)S(1)}, bf16[8,256,2048]{2,1,0:T(8,128)(2,1)S(1)}, bf16[8,256,128]{2,1,0:T(8,128)(2,1)S(1)}, bf16[8,256,128]{2,1...) custom-call(bf16[256,1024]{1,0:T(8,128)(2,1)} %bitcast.11, bf16[256,128]{1,0:T(8,128)(2,1)} %bitcast.14, ...), custom_call_target="tpu_custom_call" | custom-call | flops 2147483648 | bytes 16777216 | tf_op jit(solution)/shard_map/pallas_call | solution.py:300
  23.8 0.8 %shard_map.85 = (bf16[256,1024]{1,0:T(8,128)(2,1)}, f32[8,128]{1,0:T(8,128)S(1)}) custom-call(bf16[256,1024]{1,0:T(8,128)(2,1)S(1)} %get-tuple-element.15.o_ref), custom_call_target="tpu_custom_call" | custom-call | tf_op jit(solution)/shard_map/pallas_call | solution.py:331
  24.6 4.8 %collective-permute-done.cot_ref = bf16[256,1024]{1,0:T(8,128)(2,1)S(1)} collective-permute-done((bf16[256,1024]{1,0:T(8,128)(2,1)}, bf16[256,1024]{1,0:T(8,128)(2,1)S(1)}, u32[]{:S(2)}, u32[]{:S(2)}) %collective-permute-start) | collective-permute-done | bytes 524320 | tf_op jit(solution)/shard_map/ppermute | solution.py:296
  29.4 18.4 %shard_map.86 = (bf16[256,1024]{1,0:T(8,128)(2,1)S(1)}, bf16[256,128]{1,0:T(8,128)(2,1)S(1)}, bf16[256,128]{1,0:T(8,128)(2,1)S(1)}) custom-call(bf16[256,1024]{1,0:T(8,128)(2,1)S(1)} %collective-permute-done.cot_ref, bf16[8,256,2048]{2,1,0:T(8,128)(2,1)S(1)} %get-tuple-element.17.probs, bf16[8,256,128]{2,1,0:T(8,128)(2,1)S(1)} %get-tuple-element.18.kbuf, ...), custom_call_target="tpu_custom_call" | custom-call | flops 4294967296 | bytes 16777216 | tf_op jit(solution)/shard_map/pallas_call | solution.py:339
  47.8 0.8 %copy.12 = bf16[1,256,1024]{2,1,0:T(8,128)(2,1)} copy(bf16[1,256,1024]{2,1,0:T(8,128)(2,1)S(1)} %bitcast.8) | data formatting | bytes 1048576
  48.6 0.6 %copy.13 = bf16[1,256,128]{2,1,0:T(8,128)(2,1)} copy(bf16[1,256,128]{2,1,0:T(8,128)(2,1)S(1)} %bitcast.10) | data formatting | bytes 131072
  49.2 0.6 %copy.14 = bf16[1,256,128]{2,1,0:T(8,128)(2,1)} copy(bf16[1,256,128]{2,1,0:T(8,128)(2,1)S(1)} %bitcast.9) | data formatting | bytes 131072
Async XLA Ops:
  0.6 28.8 %collective-permute-start = (bf16[256,1024]{1,0:T(8,128)(2,1)}, bf16[256,1024]{1,0:T(8,128)(2,1)S(1)}, u32[]{:S(2)}, u32[]{:S(2)}) collective-permute-start(bf16[256,1024]{1,0:T(8,128)(2,1)} %bitcast.12), channel_id=1, source_target_pairs={{0,480},{32,448},{64,416},{96,384},{128,352},{160,320},{192,288},{... | collective-permute-start | bytes 1572872 | tf_op jit(solution)/shard_map/ppermute | solution.py:296

commit v5 on v4

--- a/solution.py
+++ b/solution.py
@@ -284,6 +284,15 @@
     copy.wait()
 
 
+def place_kernel(*refs):
+    count = len(refs) // 2
+    copies = [pltpu.make_async_copy(refs[i], refs[count + i], refs[-1].at[i]) for i in range(count)]
+    for c in copies:
+        c.start()
+    for c in copies:
+        c.wait()
+
+
 def local(queries, keys, values, cotangent, positions):
     q, k, v, cot = queries[0], keys[0], values[0], cotangent[0]
     q, k, v, positions = (
@@ -368,6 +377,15 @@
             collective_id=2, has_side_effects=True, vmem_limit_bytes=36 * 2**20
         ),
     )(mirrored, probs, k_all, v_all, q_st, out, inverse, done)
+    grads = (grad_q, grad_k, grad_v)
+    grad_q, grad_k, grad_v = pl.pallas_call(
+        place_kernel,
+        out_shape=tuple(jax.ShapeDtypeStruct(g.shape, g.dtype) for g in grads),
+        in_specs=[vmem] * 3,
+        out_specs=(pl.BlockSpec(memory_space=pltpu.HBM),) * 3,
+        scratch_shapes=[dma((3,))],
+        compiler_params=pltpu.CompilerParams(vmem_limit_bytes=2**20),
+    )(*grads)
     return (kept[None], grad_q[None], grad_k[None], grad_v[None])
 
 

time: 50 us -> 48.8 us (0.976)
  local copies, waits for them, and re-layouts: 2.05 us -> 0 us
  Pallas kernels: 40.4 us -> 41.2 us
    unnamed x3 -> x0, local copies, waits for them, and re-layouts: 2.05 us -> none
    pallas_call x0 -> x1, Pallas kernels: none -> 0.85 us  [local(): pl.pallas_call(place_kernel, out_shape=tuple((jax.ShapeDtypeStruct(g.shap...]
  transfers between devices with their start and end apart: 1 -> 1, of which waited for: 1 -> 1; matrix products, arithmetic and copies ran while one was open for 0% -> 0% of each run, Pallas kernels for 44% -> 45%
where the time goes in v5:
time: 48.8 us; the launch traced here: 48.6 us
  Pallas kernels  41.2 us (84%)
  waiting for transfers between devices  4.81 us (10%)
  starting transfers between devices  1.92 us (4%)
  between operations  0.66 us (1%)
    pallas_call x1, Pallas kernels, local(): pl.pallas_call(functools.partial(fwd_kernel, heads, tok), out_shape=(jax....  21.2 us
    pallas_call x1, Pallas kernels, local(): pl.pallas_call(functools.partial(bwd_kernel, heads, tok), out_shape=(jax....  18.4 us
    ppermute x1, waiting for transfers between devices, local(): lax.ppermute(cot, 'section', [(s, count - 1 - s) for s in range(count)])  4.81 us
    ppermute x1, starting transfers between devices, local(): lax.ppermute(cot, 'section', [(s, count - 1 - s) for s in range(count)])  1.92 us
  transfers between devices with their start and end apart: 1, of which 1 were waited for; matrix products, arithmetic and copies ran while one was open for 0% of the time, Pallas kernels for 45%

profile of v5, /device:TPU:160, one launch (start us, length us, event | category | flops | bytes accessed | tf_op | source)
XLA Modules:
  0.0 48.6 jit_solution(9958335780967547448)
XLA Ops:
  0.6 1.9 %collective-permute-start = (bf16[256,1024]{1,0:T(8,128)(2,1)}, bf16[256,1024]{1,0:T(8,128)(2,1)S(1)}, u32[]{:S(2)}, u32[]{:S(2)}) collective-permute-start(bf16[256,1024]{1,0:T(8,128)(2,1)} %bitcast.9), channel_id=1, source_target_pairs={{0,480},{32,448},{64,416},{96,384},{128,352},{160,320},{192,288},{... | collective-permute-start | bytes 1572872 | tf_op jit(solution)/shard_map/ppermute | solution.py:305
  2.6 21.2 %shard_map.84 = (bf16[256,1024]{1,0:T(8,128)(2,1)S(1)}, bf16[8,256,2048]{2,1,0:T(8,128)(2,1)S(1)}, bf16[8,256,128]{2,1,0:T(8,128)(2,1)S(1)}, bf16[8,256,128]{2,1...) custom-call(bf16[256,1024]{1,0:T(8,128)(2,1)} %bitcast.8, bf16[256,128]{1,0:T(8,128)(2,1)} %bitcast.12, ...), custom_call_target="tpu_custom_call" | custom-call | flops 2147483648 | bytes 16777216 | tf_op jit(solution)/shard_map/pallas_call | solution.py:309
  23.8 0.8 %shard_map.85 = (bf16[256,1024]{1,0:T(8,128)(2,1)}, f32[8,128]{1,0:T(8,128)S(1)}) custom-call(bf16[256,1024]{1,0:T(8,128)(2,1)S(1)} %get-tuple-element.18.o_ref), custom_call_target="tpu_custom_call" | custom-call | tf_op jit(solution)/shard_map/pallas_call | solution.py:340
  24.6 4.8 %collective-permute-done.cot_ref = bf16[256,1024]{1,0:T(8,128)(2,1)S(1)} collective-permute-done((bf16[256,1024]{1,0:T(8,128)(2,1)}, bf16[256,1024]{1,0:T(8,128)(2,1)S(1)}, u32[]{:S(2)}, u32[]{:S(2)}) %collective-permute-start) | collective-permute-done | bytes 524320 | tf_op jit(solution)/shard_map/ppermute | solution.py:305
  29.4 18.4 %shard_map.86 = (bf16[256,1024]{1,0:T(8,128)(2,1)S(1)}, bf16[256,128]{1,0:T(8,128)(2,1)S(1)}, bf16[256,128]{1,0:T(8,128)(2,1)S(1)}) custom-call(bf16[256,1024]{1,0:T(8,128)(2,1)S(1)} %collective-permute-done.cot_ref, bf16[8,256,2048]{2,1,0:T(8,128)(2,1)S(1)} %get-tuple-element.20.probs, bf16[8,256,128]{2,1,0:T(8,128)(2,1)S(1)} %get-tuple-element.21.kbuf, ...), custom_call_target="tpu_custom_call" | custom-call | flops 4294967296 | bytes 16777216 | tf_op jit(solution)/shard_map/pallas_call | solution.py:348
  47.8 0.9 %shard_map.87 = (bf16[256,1024]{1,0:T(8,128)(2,1)}, bf16[256,128]{1,0:T(8,128)(2,1)}, bf16[256,128]{1,0:T(8,128)(2,1)}) custom-call(bf16[256,1024]{1,0:T(8,128)(2,1)S(1)} %get-tuple-element.26.refs_0_, bf16[256,128]{1,0:T(8,128)(2,1)S(1)} %get-tuple-element.27.refs_1_, bf16[256,128]{1,0:T(8,128)(2,1)S(1)} %get-tuple-element.28.refs_2_), custom_call_target="tpu_custom_call" | custom-call | tf_op jit(solution)/shard_map/pallas_call | solution.py:381
Async XLA Ops:
  0.6 28.8 %collective-permute-start = (bf16[256,1024]{1,0:T(8,128)(2,1)}, bf16[256,1024]{1,0:T(8,128)(2,1)S(1)}, u32[]{:S(2)}, u32[]{:S(2)}) collective-permute-start(bf16[256,1024]{1,0:T(8,128)(2,1)} %bitcast.9), channel_id=1, source_target_pairs={{0,480},{32,448},{64,416},{96,384},{128,352},{160,320},{192,288},{... | collective-permute-start | bytes 1572872 | tf_op jit(solution)/shard_map/ppermute | solution.py:305
